TPU v7x, 32 devices: a whole 2x2x4 slice. The times are simulated.
32 devices in a mesh: seq: 8 (over z, x), fsdp: 4 (over y, core).
Axes of the slice: x: 2, y: 2, z: 4, core: 2. Of those that a mesh axis runs over, the one named last changes fastest.
Arguments:
- tokens: bfloat16 [4096, 1536], P(('seq', 'fsdp')), may hold values from -6 to 6
- cotangent: bfloat16 [4096, 1536], P(('seq', 'fsdp')), may hold values from -6 to 6
- lengths: int32 [7], replicated, may hold values from 1 to 3585, 4096 in all
- attn_gain: bfloat16 [1536], P(('seq', 'fsdp')), may hold values from 0.5 to 1.5
- q_weight: bfloat16 [1536, 1536], P(('seq', 'fsdp')), may hold values from -0.15625 to 0.15625
- q_bias: bfloat16 [1536], P(('seq', 'fsdp')), may hold values from -3 to 3
- k_weight: bfloat16 [1536, 256], P(('seq', 'fsdp')), may hold values from -0.15625 to 0.15625
- k_bias: bfloat16 [256], P(('seq', 'fsdp')), may hold values from -3 to 3
- v_weight: bfloat16 [1536, 256], P(('seq', 'fsdp')), may hold values from -0.15625 to 0.15625
- v_bias: bfloat16 [256], P(('seq', 'fsdp')), may hold values from -3 to 3
- o_weight: bfloat16 [1536, 1536], P(('seq', 'fsdp')), may hold values from -1.25 to 1.25
- mlp_gain: bfloat16 [1536], P(('seq', 'fsdp')), may hold values from 0.5 to 1.5
- gate_weight: bfloat16 [1536, 8960], P(('seq', 'fsdp')), may hold values from -0.15625 to 0.15625
- up_weight: bfloat16 [1536, 8960], P(('seq', 'fsdp')), may hold values from -0.15625 to 0.15625
- down_weight: bfloat16 [8960, 1536], P(('seq', 'fsdp')), may hold values from -0.0625 to 0.0625
Outputs:
- layer_out: bfloat16 [4096, 1536], P(('seq', 'fsdp'))
- input_grad: float32 [4096, 1536], P(('seq', 'fsdp'))
- attn_gain_grad: float32 [1536], P(('seq', 'fsdp'))
- q_weight_grad: float32 [1536, 1536], P(('seq', 'fsdp'))
- q_bias_grad: float32 [1536], P(('seq', 'fsdp'))
- k_weight_grad: float32 [1536, 256], P(('seq', 'fsdp'))
- k_bias_grad: float32 [256], P(('seq', 'fsdp'))
- v_weight_grad: float32 [1536, 256], P(('seq', 'fsdp'))
- v_bias_grad: float32 [256], P(('seq', 'fsdp'))
- o_weight_grad: float32 [1536, 1536], P(('seq', 'fsdp'))
- mlp_gain_grad: float32 [1536], P(('seq', 'fsdp'))
- gate_weight_grad: float32 [1536, 8960], P(('seq', 'fsdp'))
- up_weight_grad: float32 [1536, 8960], P(('seq', 'fsdp'))
- down_weight_grad: float32 [8960, 1536], P(('seq', 'fsdp'))
Inputs may be any that keep to these rules, and one draw needn't show every extreme that they name: The lengths of the 7 packed sequences in order; they sum to 4096 and the longest has exactly 3585 tokens.
All inputs are finite; a program needn't handle non-finite values.
Results may differ from a plain program's by a relative error of at most 0.02.
Values may be sent and summed in bfloat16 or wider, within the bound.
A program may use at most 896 MiB of HBM per device.

v0:
```python
import functools

import jax
import jax.numpy as jnp
import numpy as np
from jax import lax
from jax.experimental import pallas as pl
from jax.experimental.pallas import tpu as pltpu
from jax.sharding import PartitionSpec as P

HEADS = 12
KV_HEADS = 2
HEAD_DIM = 128
GROUP = HEADS // KV_HEADS
EPSILON = 1e-06
ROPE_BASE = 10000.0
LOG2E = 1.4426950408889634
AXES = ("seq", "fsdp")
VMEM_LIMIT = 56 << 20
VMEM_JOINED = 60 << 20
F32 = jnp.float32
BF16 = jnp.bfloat16
DMA = pltpu.SemaphoreType.DMA


class Place:
    def __init__(self, depth):
        self.depth = depth
        self.s = lax.axis_index("seq")
        self.f = lax.axis_index("fsdp")
        self.z = lax.div(self.s, 2)
        self.x = lax.rem(self.s, 2)
        self.y = lax.div(self.f, 2)
        self.c = lax.rem(self.f, 2)
        self.up = self.z + 1 < depth
        self.down = self.z > 0

    def flip_x(self):
        return (self.s + 1 - 2 * self.x, self.f)

    def flip_y(self):
        return (self.s, self.f + 2 - 4 * self.y)

    def flip_c(self):
        return (self.s, self.f + 1 - 2 * self.c)

    def z_up(self):
        return (self.s + 2, self.f)

    def z_down(self):
        return (self.s - 2, self.f)

    def first(self):
        return (
            self.s + (1 - self.c) * (1 - 2 * self.x),
            self.f + self.c * (2 - 4 * self.y),
        )

    def second(self):
        return (
            self.s + self.c * (1 - 2 * self.x),
            self.f + (1 - self.c) * (2 - 4 * self.y),
        )

    def corner(self, i, j):
        over_x = i * (1 - self.c) + j * self.c
        over_y = j * (1 - self.c) + i * self.c
        return (self.x + over_x * (1 - 2 * self.x), self.y + over_y * (1 - 2 * self.y))

    def wave(self, k):
        if k == 0:
            return [(self.z, None)]
        return [(self.z - k, self.z - k >= 0), (self.z + k, self.z + k < self.depth)]


def guard(condition, body):
    if condition is None:
        body()
    else:
        pl.when(condition)(body)


def both(one, other):
    return one if other is None else jnp.logical_and(one, other)


def greet(place, others=()):
    barrier = pltpu.get_barrier_semaphore()
    partners = [place.flip_x(), place.flip_y(), place.flip_c(), *others]
    for partner in partners:
        pl.semaphore_signal(barrier, inc=1, device_id=partner, device_id_type=pl.DeviceIdType.MESH)

    def tell_up():
        pl.semaphore_signal(
            barrier, inc=1, device_id=place.z_up(), device_id_type=pl.DeviceIdType.MESH
        )

    def tell_down():
        pl.semaphore_signal(
            barrier, inc=1, device_id=place.z_down(), device_id_type=pl.DeviceIdType.MESH
        )

    pl.when(place.up)(tell_up)
    pl.when(place.down)(tell_down)
    pl.semaphore_wait(
        barrier, len(partners) + place.up.astype(jnp.int32) + place.down.astype(jnp.int32)
    )


def remote(src, dst, send_sem, recv_sem, device):
    return pltpu.make_async_remote_copy(
        src_ref=src,
        dst_ref=dst,
        send_sem=send_sem,
        recv_sem=recv_sem,
        device_id=device,
        device_id_type=pl.DeviceIdType.MESH,
    )


def add_into(target, term, rows):
    step = rows if rows <= 48 else (32 if rows % 32 == 0 else 16)

    def body(number, carry):
        at = pl.ds(pl.multiple_of(number * step, step), step)
        target[at, :] = (target[at, :].astype(F32) + term[at, :].astype(F32)).astype(BF16)
        return carry

    lax.fori_loop(0, rows // step, body, 0)


class Gather:
    def __init__(self, place, wide, own, out, sems, mixed=False):
        self.place, self.wide, self.own, self.out, self.sems = place, wide, own, out, sems
        self.mixed = mixed
        self.sent = []

    @staticmethod
    def semaphores(depth, wide, mixed=False):
        base = [DMA((1,)), DMA((2 * depth,)), DMA((depth,)), DMA((depth,)), DMA((depth,))]
        if mixed:
            base += [DMA((2 * depth,)), DMA((depth,))]
        if wide:
            base += [DMA((2 * depth,)), DMA((2 * depth,)), DMA((4 * depth,)), DMA((4 * depth,))]
        return base

    def at(self, zi, i, j):
        place = self.place
        if self.wide:
            x, y = place.corner(i, j)
            return self.out.at[zi, x, y, place.c]
        return self.out.at[zi, place.x + i * (1 - 2 * place.x)]

    def send(self, src, dst, send_sem, recv_sem, device, condition):
        copy = remote(src, dst, send_sem, recv_sem, device)
        guard(condition, copy.start)
        self.sent.append((copy, condition))

    def local(self):
        copy = pltpu.make_async_copy(
            self.own, self.at(self.place.z, 0, 0), self.sems[0].at[0]
        )
        return copy

    def along(self, k, zi, side, ok, column, z_send, z_recv, source=None):
        place, depth = self.place, self.place.depth
        block = self.at(zi, column, 0)
        source = block if source is None else source
        if k == 0 or side == 0:
            self.send(
                source, block, z_send.at[k], z_recv.at[zi], place.z_up(), both(place.up, ok)
            )
        if k == 0 or side == 1:
            self.send(
                source,
                block,
                z_send.at[depth + k],
                z_recv.at[zi],
                place.z_down(),
                both(place.down, ok),
            )

    def arrive(self, k):
        place = self.place
        z_send, z_recv, a_send, a_recv = self.sems[1:5]
        across = place.first() if self.wide else place.flip_x()
        for side, (zi, ok) in enumerate(place.wave(k)):
            block = self.at(zi, 0, 0)
            source = self.own if k == 0 else block
            if k > 0:
                landed = remote(block, block, z_send.at[0], z_recv.at[zi], place.z_up())
                guard(ok, landed.wait_recv)
            self.along(k, zi, side, ok, 0, z_send, z_recv, source)
            crossing = both(place.c == 0, ok) if self.mixed and k > 0 else ok
            self.send(source, block, a_send.at[zi], a_recv.at[zi], across, crossing)
            if self.wide:
                b_send, b_recv = self.sems[5:7]
                self.send(
                    source, block, b_send.at[2 * zi], b_recv.at[2 * zi], place.second(), ok
                )

    def across(self, k):
        place = self.place
        a_send, a_recv = self.sems[3:5]
        for side, (zi, ok) in enumerate(place.wave(k)):
            block = self.at(zi, 1, 0)
            crossing = both(place.c == 0, ok) if self.mixed and k > 0 else ok
            landed = remote(block, block, a_send.at[0], a_recv.at[zi], place.first())
            guard(crossing, landed.wait_recv)
            if self.mixed:
                z_send, z_recv = self.sems[5:7]
                carried = both(place.c == 1, ok)
                if k > 0:
                    landed = remote(block, block, z_send.at[0], z_recv.at[zi], place.z_up())
                    guard(carried, landed.wait_recv)
                self.along(k, zi, side, carried, 1, z_send, z_recv)
            if self.wide:
                b_send, b_recv = self.sems[5:7]
                self.send(
                    block, block, b_send.at[2 * zi + 1], b_recv.at[2 * zi + 1], place.second(), ok
                )

    def hand(self, k):
        place = self.place
        b_send, b_recv, c_send, c_recv = self.sems[5:9]
        for zi, ok in place.wave(k):
            for i in range(2):
                block = self.at(zi, i, 1)
                landed = remote(block, block, b_send.at[0], b_recv.at[2 * zi + i], place.second())
                guard(ok, landed.wait_recv)
            for x in range(2):
                for y in range(2):
                    block = self.out.at[zi, x, y, place.c]
                    slot = 4 * zi + 2 * x + y
                    self.send(
                        block, block, c_send.at[slot], c_recv.at[slot], place.flip_c(), ok
                    )

    def take(self, k):
        place = self.place
        c_send, c_recv = self.sems[7:9]
        for zi, ok in place.wave(k):
            for x in range(2):
                for y in range(2):
                    block = self.out.at[zi, x, y, 1 - place.c]
                    slot = 4 * zi + 2 * x + y
                    landed = remote(block, block, c_send.at[0], c_recv.at[slot], place.flip_c())
                    guard(ok, landed.wait_recv)

    def settle(self):
        for copy, condition in self.sent:
            guard(condition, copy.wait_send)


def drive_gathers(place, gathers):
    depth = place.depth
    locals_ = [gather.local() for gather in gathers]
    for copy in locals_:
        copy.start()
    for step in range(depth + 3):
        for gather in gathers:
            if step < depth:
                gather.arrive(step)
        if step == 0:
            for copy in locals_:
                copy.wait()
        for gather in gathers:
            if 0 <= step - 1 < depth:
                gather.across(step - 1)
        for gather in gathers:
            if gather.wide and 0 <= step - 2 < depth:
                gather.hand(step - 2)
        for gather in gathers:
            if gather.wide and 0 <= step - 3 < depth:
                gather.take(step - 3)
    for gather in gathers:
        gather.settle()


def gather_shape(depth, wide, own):
    lead = (depth, 2, 2, 2) if wide else (depth, 2)
    return jax.ShapeDtypeStruct(lead + own.shape, own.dtype)


def call_gathers(depth, collective_id, wides, owns):
    def kernel(*refs):
        count = len(owns)
        place = Place(depth)
        greet(place)
        gathers, used = [], 2 * count
        for number, wide in enumerate(wides):
            need = len(Gather.semaphores(depth, wide))
            gathers.append(
                Gather(place, wide, refs[number], refs[count + number], refs[used : used + need])
            )
            used += need
        drive_gathers(place, gathers)

    scratch = []
    for wide in wides:
        scratch += Gather.semaphores(depth, wide)
    return pl.pallas_call(
        kernel,
        out_shape=[gather_shape(depth, wide, own) for wide, own in zip(wides, owns)],
        in_specs=[pl.BlockSpec(memory_space=pl.ANY)] * len(owns),
        out_specs=[pl.BlockSpec(memory_space=pl.ANY)] * len(owns),
        scratch_shapes=scratch,
        compiler_params=pltpu.CompilerParams(
            collective_id=collective_id, has_side_effects=True, vmem_limit_bytes=VMEM_LIMIT
        ),
    )(*owns)


def start_kernel(depth, *refs):
    (pack, cot, wide_in, down_in, pack_out, cot_out, wide_out, down_out), sems = refs[:8], refs[8:]
    place = Place(depth)
    count = 2 * depth
    partners = []
    for offset in range(1, count):
        partners.append((lax.rem(place.s + offset, count), place.f))
    greet(place, partners)
    first = len(Gather.semaphores(depth, True))
    second = first + len(Gather.semaphores(depth, False))
    gathers = [
        Gather(place, True, pack, pack_out, sems[:first]),
        Gather(place, False, cot, cot_out, sems[first:second]),
    ]
    local_sem, e_send, e_recv, y_send, y_recv, c_send, c_recv, d_sem, d_send, d_recv = sems[second:]
    sent = []

    def send(src, dst, send_sem, recv_sem, device):
        copy = remote(src, dst, send_sem, recv_sem, device)
        copy.start()
        sent.append(copy)

    locals_ = [gather.local() for gather in gathers]
    locals_.append(
        pltpu.make_async_copy(
            wide_in.at[:, place.s], wide_out.at[:, place.s, place.f], local_sem.at[0]
        )
    )
    locals_.append(pltpu.make_async_copy(down_in, down_out.at[place.f], d_sem.at[0]))
    for copy in locals_:
        copy.start()

    y_f = place.f + 2 - 4 * place.y
    c_f = place.f + 1 - 2 * place.c
    yc_f = y_f + 1 - 2 * place.c

    def exchange(offset):
        to = lax.rem(place.s + offset, count)
        send(
            wide_in.at[:, to],
            wide_out.at[:, place.s, place.f],
            e_send.at[offset],
            e_recv.at[offset],
            (to, place.f),
        )

    def onward(offset):
        origin = lax.rem(place.s + count - offset, count)
        block = wide_out.at[:, origin, place.f]
        if offset > 0:
            remote(block, block, e_send.at[0], e_recv.at[offset], place.flip_y()).wait_recv()
        send(block, block, y_send.at[offset], y_recv.at[offset], place.flip_y())
        send(block, block, c_send.at[2 * offset], c_recv.at[2 * offset], place.flip_c())

    def sideways(offset):
        origin = lax.rem(place.s + count - offset, count)
        block = wide_out.at[:, origin, y_f]
        remote(block, block, y_send.at[0], y_recv.at[offset], place.flip_y()).wait_recv()
        send(block, block, c_send.at[2 * offset + 1], c_recv.at[2 * offset + 1], place.flip_c())

    def last(offset):
        origin = lax.rem(place.s + count - offset, count)
        for slot, owner in ((2 * offset, c_f), (2 * offset + 1, yc_f)):
            block = wide_out.at[:, origin, owner]
            remote(block, block, c_send.at[0], c_recv.at[slot], place.flip_c()).wait_recv()

    for gather in gathers:
        gather.arrive(0)
    send(down_in, down_out.at[place.f], d_send.at[0], d_recv.at[0], place.flip_y())
    send(down_in, down_out.at[place.f], d_send.at[1], d_recv.at[1], place.flip_c())
    for offset in range(1, count):
        exchange(offset)
    for copy in locals_:
        copy.wait()
    onward(0)
    total = depth + 3
    for step in range(1, total):
        for gather in gathers:
            if step < depth:
                gather.arrive(step)
        for gather in gathers:
            if 0 <= step - 1 < depth:
                gather.across(step - 1)
        for gather in gathers:
            if gather.wide and 0 <= step - 2 < depth:
                gather.hand(step - 2)
        for gather in gathers:
            if gather.wide and 0 <= step - 3 < depth:
                gather.take(step - 3)
    block = down_out.at[y_f]
    remote(block, block, d_send.at[0], d_recv.at[0], place.flip_y()).wait_recv()
    send(block, block, d_send.at[2], d_recv.at[2], place.flip_c())
    for offset in range(1, count):
        onward(offset)
        sideways(offset - 1)
    sideways(count - 1)
    for offset in range(count):
        last(offset)
    for slot, owner in ((1, c_f), (2, yc_f)):
        block = down_out.at[owner]
        remote(block, block, d_send.at[0], d_recv.at[slot], place.flip_c()).wait_recv()
    for gather in gathers:
        gather.settle()
    for copy in sent:
        copy.wait_send()


def call_start(depth, collective_id, pack, cot, wide, down):
    count = 2 * depth
    _, _, rows, columns = wide.shape
    scratch = Gather.semaphores(depth, True) + Gather.semaphores(depth, False)
    scratch += [DMA((1,)), DMA((count,)), DMA((count,)), DMA((count,)), DMA((count,))]
    scratch += [DMA((2 * count,)), DMA((2 * count,)), DMA((1,)), DMA((3,)), DMA((3,))]
    return pl.pallas_call(
        functools.partial(start_kernel, depth),
        out_shape=[
            gather_shape(depth, True, pack),
            gather_shape(depth, False, cot),
            jax.ShapeDtypeStruct((2, count, 4, rows, columns), BF16),
            jax.ShapeDtypeStruct((4,) + down.shape, BF16),
        ],
        in_specs=[pl.BlockSpec(memory_space=pl.ANY)] * 4,
        out_specs=[pl.BlockSpec(memory_space=pl.ANY)] * 4,
        scratch_shapes=scratch,
        compiler_params=pltpu.CompilerParams(
            collective_id=collective_id, has_side_effects=True, vmem_limit_bytes=VMEM_LIMIT
        ),
    )(pack, cot, wide, down)


class Reduce:
    def __init__(self, place, wide, rows, own, out, buffers, sems, near=None, causal=False):
        self.place, self.wide, self.rows = place, wide, rows
        self.own, self.out, self.buffers, self.sems = own, out, buffers, sems
        self.near = near
        self.causal = causal
        self.sent = []

    def wave(self, k):
        waves = self.place.wave(k)
        return waves[:1] if self.causal else waves

    def near_block(self, zi):
        return self.own.at[zi, self.place.x] if self.near is None else self.near.at[zi]

    @staticmethod
    def scratch(depth, wide, block):
        buffers = [
            pltpu.VMEM((depth,) + block, BF16),
            pltpu.VMEM((depth + 1,) + block, BF16),
        ]
        sems = [DMA((depth,)), DMA((depth,)), DMA((2 * depth,)), DMA((2 * depth,))]
        if wide:
            buffers += [
                pltpu.VMEM((depth, 2, 2) + block, BF16),
                pltpu.VMEM((depth, 2) + block, BF16),
            ]
            sems += [DMA((4 * depth,)), DMA((4 * depth,)), DMA((2 * depth,)), DMA((2 * depth,))]
        return buffers, sems

    def send(self, src, dst, send_sem, recv_sem, device, condition):
        copy = remote(src, dst, send_sem, recv_sem, device)
        guard(condition, copy.start)
        self.sent.append((copy, condition))

    def cores(self, k):
        place = self.place
        c_send, c_recv = self.sems[4:6]
        got = self.buffers[2]
        for zi, ok in self.wave(k):
            for x in range(2):
                for y in range(2):
                    slot = 4 * zi + 2 * x + y
                    self.send(
                        self.own.at[zi, x, y, 1 - place.c],
                        got.at[zi, x, y],
                        c_send.at[slot],
                        c_recv.at[slot],
                        place.flip_c(),
                        ok,
                    )

    def over_second(self, k):
        place = self.place
        c_send, c_recv, b_send, b_recv = self.sems[4:8]
        got, next_ = self.buffers[2:4]
        for zi, ok in self.wave(k):

            def body(zi=zi):
                for j in (1, 0):
                    for i in (1, 0):
                        x, y = place.corner(i, j)
                        block = got.at[zi, x, y]
                        slot = 4 * zi + 2 * x + y
                        remote(
                            block, block, c_send.at[0], c_recv.at[slot], place.flip_c()
                        ).wait_recv()
                        add_into(block, self.own.at[zi, x, y, place.c], self.rows)
                        if j == 1:
                            remote(
                                block,
                                next_.at[zi, i],
                                b_send.at[2 * zi + i],
                                b_recv.at[2 * zi + i],
                                place.second(),
                            ).start()

            guard(ok, body)
            for i in (1, 0):
                x, y = place.corner(i, 1)
                copy = remote(
                    got.at[zi, x, y],
                    next_.at[zi, i],
                    b_send.at[2 * zi + i],
                    b_recv.at[2 * zi + i],
                    place.second(),
                )
                self.sent.append((copy, ok))

    def over_first(self, k):
        place = self.place
        a_send, a_recv = self.sems[0:2]
        got = self.buffers[0]
        for zi, ok in self.wave(k):
            if self.wide:
                b_send, b_recv = self.sems[6:8]
                before, held = self.buffers[2:4]

                def body(zi=zi):
                    for i in (1, 0):
                        block = held.at[zi, i]
                        x, y = place.corner(i, 0)
                        remote(
                            block, block, b_send.at[0], b_recv.at[2 * zi + i], place.second()
                        ).wait_recv()
                        add_into(block, before.at[zi, x, y], self.rows)
                        if i == 1:
                            remote(
                                block, got.at[zi], a_send.at[zi], a_recv.at[zi], place.first()
                            ).start()

                guard(ok, body)
                copy = remote(
                    held.at[zi, 1], got.at[zi], a_send.at[zi], a_recv.at[zi], place.first()
                )
                self.sent.append((copy, ok))
            else:
                self.send(
                    self.own.at[zi, 1 - place.x],
                    got.at[zi],
                    a_send.at[zi],
                    a_recv.at[zi],
                    place.flip_x(),
                    ok,
                )

    def cross_copy(self, zi):
        place = self.place
        return remote(
            self.own.at[zi, 1 - place.x],
            self.buffers[0].at[zi],
            self.sems[0].at[zi],
            self.sems[1].at[zi],
            place.flip_x(),
        )

    def cross(self, zi):
        self.cross_copy(zi).start()

    def crossed(self):
        for zi in range(self.place.depth):
            self.sent.append((self.cross_copy(zi), None))

    def along(self, k):
        place, depth = self.place, self.place.depth
        a_send, a_recv, z_send, z_recv = self.sems[0:4]
        held, line = self.buffers[0:2]
        for side, (zi, ok) in enumerate(self.wave(k)):
            block = held.at[zi]

            def body(zi=zi, side=side, block=block):
                remote(block, block, a_send.at[0], a_recv.at[zi], place.first()).wait_recv()
                if self.wide:
                    add_into(block, self.buffers[3].at[zi, 0], self.rows)
                else:
                    add_into(block, self.near_block(zi), self.rows)

                def more(direction):
                    slot = direction * depth + zi
                    term = line.at[depth if k == 0 and direction == 1 else zi]
                    remote(term, term, z_send.at[0], z_recv.at[slot], place.z_up()).wait_recv()
                    add_into(block, term, self.rows)

                def pass_on(direction, to):
                    slot = direction * depth + zi
                    there = line.at[depth if k == 1 and direction == 1 else zi]
                    remote(block, there, z_send.at[slot], z_recv.at[slot], to).start()

                if k == 0:
                    if not self.causal:
                        pl.when(place.down)(functools.partial(more, 0))
                    pl.when(place.up)(functools.partial(more, 1))
                elif side == 0:
                    pl.when(place.up)(functools.partial(more, 1))
                    pass_on(1, place.z_down())
                else:
                    pl.when(place.down)(functools.partial(more, 0))
                    pass_on(0, place.z_up())

            guard(ok, body)
            if k > 0:
                direction = 1 - side
                slot = direction * depth + zi
                to = place.z_up() if side == 1 else place.z_down()
                there = line.at[depth if k == 1 and direction == 1 else zi]
                copy = remote(block, there, z_send.at[slot], z_recv.at[slot], to)
                self.sent.append((copy, ok))

    def finish(self):
        self.out[...] = self.buffers[0][self.place.z].astype(self.out.dtype)

    def settle(self):
        for copy, condition in self.sent:
            guard(condition, copy.wait_send)


def drive_reduces(place, reduces):
    depth = place.depth
    order = list(range(depth - 1, -1, -1))
    for reduce in reduces:
        for k in order:
            reduce.cores(k) if reduce.wide else reduce.over_first(k)
    for step in range(depth + 2):
        for reduce in reduces:
            if not reduce.wide:
                if step < depth:
                    reduce.along(order[step])
                continue
            if step < depth:
                reduce.over_second(order[step])
            if 0 <= step - 1 < depth:
                reduce.over_first(order[step - 1])
            if 0 <= step - 2 < depth:
                reduce.along(order[step - 2])
    for reduce in reduces:
        reduce.finish()
    for reduce in reduces:
        reduce.settle()


def call_reduces(depth, collective_id, wides, owns):
    count = len(owns)
    blocks = [own.shape[-2:] for own in owns]
    parts = [Reduce.scratch(depth, wide, block) for wide, block in zip(wides, blocks)]
    scratch = []
    for buffers, sems in parts:
        scratch += buffers + sems

    def kernel(*refs):
        place = Place(depth)
        greet(place)
        reduces, used = [], 2 * count
        for number, (buffers, sems) in enumerate(parts):
            middle, end = used + len(buffers), used + len(buffers) + len(sems)
            reduces.append(
                Reduce(
                    place,
                    wides[number],
                    blocks[number][0],
                    refs[number],
                    refs[count + number],
                    refs[used:middle],
                    refs[middle:end],
                )
            )
            used = end
        drive_reduces(place, reduces)

    return pl.pallas_call(
        kernel,
        out_shape=[jax.ShapeDtypeStruct(block, F32) for block in blocks],
        in_specs=[pl.BlockSpec(memory_space=pltpu.VMEM)] * count,
        out_specs=[pl.BlockSpec(memory_space=pltpu.VMEM)] * count,
        scratch_shapes=scratch,
        compiler_params=pltpu.CompilerParams(
            collective_id=collective_id, has_side_effects=True, vmem_limit_bytes=VMEM_LIMIT
        ),
    )(*owns)


def end_kernel(depth, shapes, *refs):
    pack, wide, down, pack_out, wide_out, down_out = refs[:6]
    block, wide_block, down_block = shapes
    buffers, sems = Reduce.scratch(depth, True, block)
    used = 6 + len(buffers)
    place = Place(depth)
    count = 2 * depth
    partners = []
    for offset in range(1, count):
        partners.append((lax.rem(place.s + offset, count), place.f))
    greet(place, partners)
    reduce = Reduce(
        place, True, block[0], pack, pack_out, refs[6:used], refs[used : used + len(sems)]
    )
    used += len(sems)
    w_core, w_y, d_core, d_y = refs[used : used + 4]
    wc_send, wc_recv, wy_send, wy_recv, e_send, e_recv, e_sem = refs[used + 4 : used + 11]
    dc_send, dc_recv, dy_send, dy_recv = refs[used + 11 :]
    sent = []
    wide_rows, down_rows = wide_block[1], down_block[0]

    def send(src, dst, send_sem, recv_sem, device):
        copy = remote(src, dst, send_sem, recv_sem, device)
        copy.start()
        sent.append(copy)

    def landed(ref, recv_sem):
        remote(ref, ref, e_send.at[0], recv_sem, place.flip_c()).wait_recv()

    mine_y, other_y = place.y, 1 - place.y
    offsets = list(range(1, count)) + [0]
    for y in range(2):
        side = other_y if y == 0 else mine_y
        send(
            down.at[2 * side + 1 - place.c],
            d_core.at[side],
            dc_send.at[side],
            dc_recv.at[side],
            place.flip_c(),
        )
    for offset in offsets:
        to = lax.rem(place.s + offset, count)
        for y in range(2):
            send(
                wide.at[:, to, 2 * y + 1 - place.c],
                w_core.at[y, offset],
                wc_send.at[2 * offset + y],
                wc_recv.at[2 * offset + y],
                place.flip_c(),
            )
    order = list(range(depth - 1, -1, -1))
    for k in order:
        reduce.cores(k)

    def wide_add(target, term):
        for part in range(2):
            add_into(target.at[part], term.at[part], wide_rows)

    def wide_cores(offset):
        to = lax.rem(place.s + offset, count)
        for side in (other_y, mine_y):
            landed(w_core.at[side, offset], wc_recv.at[2 * offset + side])
            wide_add(w_core.at[side, offset], wide.at[:, to, 2 * side + place.c])
            if side is other_y:
                send(
                    w_core.at[side, offset],
                    w_y.at[offset],
                    wy_send.at[offset],
                    wy_recv.at[offset],
                    place.flip_y(),
                )

    def wide_across(offset):
        landed(w_y.at[offset], wy_recv.at[offset])
        wide_add(w_y.at[offset], w_core.at[mine_y, offset])
        to = lax.rem(place.s + offset, count)
        if offset > 0:
            send(
                w_y.at[offset],
                wide_out.at[place.s],
                e_send.at[offset],
                e_recv.at[offset],
                (to, place.f),
            )
        else:
            pltpu.make_async_copy(w_y.at[0], wide_out.at[place.s], e_sem.at[0]).start()

    for offset in offsets[: count // 2]:
        wide_cores(offset)
    for step in range(depth):
        reduce.over_second(order[step])
        if step >= 1:
            reduce.over_first(order[step - 1])
        if step == 0:
            for offset in offsets[count // 2 :]:
                wide_cores(offset)
            for side in (other_y, mine_y):
                landed(d_core.at[side], dc_recv.at[side])
                add_into(d_core.at[side], down.at[2 * side + place.c], down_rows)
                if side is other_y:
                    send(d_core.at[side], d_y.at[0], dy_send.at[0], dy_recv.at[0], place.flip_y())
        for offset in offsets[step * count // depth : (step + 1) * count // depth]:
            wide_across(offset)
        if step >= 2:
            reduce.along(order[step - 2])
    reduce.over_first(order[depth - 1])
    for step in range(max(depth - 2, 0), depth):
        reduce.along(order[step])
    reduce.finish()
    landed(d_y.at[0], dy_recv.at[0])
    down_out[...] = d_y[0].astype(F32) + d_core[mine_y].astype(F32)
    for offset in range(1, count):
        origin = lax.rem(place.s + count - offset, count)
        landed(wide_out.at[origin], e_recv.at[offset])
    pltpu.make_async_copy(w_y.at[0], wide_out.at[place.s], e_sem.at[0]).wait()
    reduce.settle()
    for copy in sent:
        copy.wait_send()


def call_end(depth, collective_id, pack, wide, down):
    count = 2 * depth
    block = pack.shape[-2:]
    wide_block = (2,) + wide.shape[-2:]
    down_block = down.shape[-2:]
    buffers, sems = Reduce.scratch(depth, True, block)
    scratch = buffers + sems
    scratch += [
        pltpu.VMEM((2, count) + wide_block, BF16),
        pltpu.VMEM((count,) + wide_block, BF16),
        pltpu.VMEM((2,) + down_block, BF16),
        pltpu.VMEM((1,) + down_block, BF16),
    ]
    scratch += [DMA((2 * count,)), DMA((2 * count,)), DMA((count,)), DMA((count,))]
    scratch += [DMA((count,)), DMA((count,)), DMA((1,))]
    scratch += [DMA((2,)), DMA((2,)), DMA((1,)), DMA((1,))]
    vmem = pl.BlockSpec(memory_space=pltpu.VMEM)
    return pl.pallas_call(
        functools.partial(end_kernel, depth, (block, wide_block, down_block)),
        out_shape=[
            jax.ShapeDtypeStruct(block, F32),
            jax.ShapeDtypeStruct((count,) + wide_block, BF16),
            jax.ShapeDtypeStruct(down_block, F32),
        ],
        in_specs=[vmem] * 3,
        out_specs=[vmem, vmem, vmem],
        scratch_shapes=scratch,
        compiler_params=pltpu.CompilerParams(
            collective_id=collective_id, has_side_effects=True, vmem_limit_bytes=VMEM_LIMIT
        ),
    )(pack, wide, down)


def forward_kernel(span, info, begin, query, key, value, mixed, lse, m_acc, l_acc, o_acc):
    rows = begin.shape[0]
    first_row, low, high = info[0], info[1], info[2]
    scale = HEAD_DIM ** (-0.5) * LOG2E
    m_acc[...] = jnp.full_like(m_acc, -1e30)
    l_acc[...] = jnp.zeros_like(l_acc)
    o_acc[...] = jnp.zeros_like(o_acc)
    places = first_row + lax.broadcasted_iota(jnp.int32, (rows, span), 0)
    offsets = lax.broadcasted_iota(jnp.int32, (rows, span), 1)

    def step(number, carry):
        base = pl.multiple_of(number * span, span)
        keys_at = base + offsets
        visible = jnp.logical_and(keys_at >= begin[...], keys_at <= places)
        for g in range(KV_HEADS):
            lanes = slice(g * HEAD_DIM, (g + 1) * HEAD_DIM)
            scores = lax.dot_general(
                query[g],
                key[pl.ds(base, span), lanes],
                (((1,), (1,)), ((), ())),
                preferred_element_type=F32,
            )
            scores = scores.reshape(GROUP, rows, span) * scale
            scores = jnp.where(visible[None], scores, -1e30).reshape(GROUP * rows, span)
            old = m_acc[g]
            new = jnp.maximum(old, jnp.max(scores, axis=-1, keepdims=True))
            weights = jnp.exp2(scores - new[:, :1])
            weights = jnp.where(
                visible[None], weights.reshape(GROUP, rows, span), 0.0
            ).reshape(GROUP * rows, span)
            fade = jnp.exp2(old - new)
            l_acc[g] = l_acc[g] * fade + jnp.sum(weights, axis=-1, keepdims=True)
            o_acc[g] = o_acc[g] * fade + jnp.dot(
                weights.astype(BF16),
                value[pl.ds(base, span), lanes],
                preferred_element_type=F32,
            )
            m_acc[g] = new
        return carry

    lax.fori_loop(low, high, step, 0)
    for g in range(KV_HEADS):
        mixed[g] = o_acc[g] / l_acc[g]
        lse[g] = m_acc[g] + jnp.log2(l_acc[g])


def call_forward(span, info, begin, query, key, value):
    stacked = query.shape[1]
    vmem = pl.BlockSpec(memory_space=pltpu.VMEM)
    return pl.pallas_call(
        functools.partial(forward_kernel, span),
        out_shape=[
            jax.ShapeDtypeStruct((KV_HEADS, stacked, HEAD_DIM), F32),
            jax.ShapeDtypeStruct((KV_HEADS, stacked, HEAD_DIM), F32),
        ],
        in_specs=[pl.BlockSpec(memory_space=pltpu.SMEM)] + [vmem] * 4,
        out_specs=[vmem, vmem],
        scratch_shapes=[pltpu.VMEM((KV_HEADS, stacked, HEAD_DIM), F32)] * 3,
        compiler_params=pltpu.CompilerParams(vmem_limit_bytes=VMEM_LIMIT),
    )(info, begin, query, key, value)


def backward_kernel(
    span, info, begin, query, key, value, mixed, lse, grad, dquery, dkeys, delta
):
    rows = begin.shape[0]
    first_row, low, high = info[0], info[1], info[2]
    scale = HEAD_DIM ** (-0.5) * LOG2E
    dquery[...] = jnp.zeros_like(dquery)
    width = KV_HEADS * HEAD_DIM
    for g in range(KV_HEADS):
        delta[g] = jnp.broadcast_to(
            jnp.sum(grad[g].astype(F32) * mixed[g], axis=-1, keepdims=True), delta.shape[1:]
        )
    places = first_row + lax.broadcasted_iota(jnp.int32, (rows, span), 0)
    offsets = lax.broadcasted_iota(jnp.int32, (rows, span), 1)

    def clear(number, carry):
        base = pl.multiple_of(number * span, span)
        dkeys[pl.ds(base, span), :] = jnp.zeros((span, dkeys.shape[1]), BF16)
        return carry

    lax.fori_loop(0, low, clear, 0)
    lax.fori_loop(high, dkeys.shape[0] // span, clear, 0)

    def step(number, carry):
        base = pl.multiple_of(number * span, span)
        keys_at = base + offsets
        visible = jnp.logical_and(keys_at >= begin[...], keys_at <= places)
        for g in range(KV_HEADS):
            lanes = slice(g * HEAD_DIM, (g + 1) * HEAD_DIM)
            key_rows = key[pl.ds(base, span), lanes]
            value_rows = value[pl.ds(base, span), lanes]
            scores = lax.dot_general(
                query[g], key_rows, (((1,), (1,)), ((), ())), preferred_element_type=F32
            )
            dprobs = lax.dot_general(
                grad[g], value_rows, (((1,), (1,)), ((), ())), preferred_element_type=F32
            )
            probs = jnp.exp2(scores * scale - lse[g][:, :1])
            probs = jnp.where(
                visible[None], probs.reshape(GROUP, rows, span), 0.0
            ).reshape(GROUP * rows, span)
            dscores = (probs * (dprobs - delta[g][:, :1])).astype(BF16)
            dquery[g] += jnp.dot(dscores, key_rows, preferred_element_type=F32)
            dkeys[pl.ds(base, span), lanes] = lax.dot_general(
                dscores, query[g], (((0,), (0,)), ((), ())), preferred_element_type=F32
            ).astype(BF16)
            dkeys[
                pl.ds(base, span), width + g * HEAD_DIM : width + (g + 1) * HEAD_DIM
            ] = lax.dot_general(
                probs.astype(BF16),
                grad[g],
                (((0,), (0,)), ((), ())),
                preferred_element_type=F32,
            ).astype(BF16)
        return carry

    lax.fori_loop(low, high, step, 0)


def call_backward(span, info, begin, query, key, value, mixed, lse, grad):
    stacked = query.shape[1]
    vmem = pl.BlockSpec(memory_space=pltpu.VMEM)
    return pl.pallas_call(
        functools.partial(backward_kernel, span),
        out_shape=[
            jax.ShapeDtypeStruct((KV_HEADS, stacked, HEAD_DIM), F32),
            jax.ShapeDtypeStruct((key.shape[0], 2 * key.shape[1]), BF16),
        ],
        in_specs=[pl.BlockSpec(memory_space=pltpu.SMEM)] + [vmem] * 7,
        out_specs=[vmem, vmem],
        scratch_shapes=[pltpu.VMEM((KV_HEADS, stacked, HEAD_DIM), F32)],
        compiler_params=pltpu.CompilerParams(vmem_limit_bytes=VMEM_LIMIT),
    )(info, begin, query, key, value, mixed, lse, grad)


class PairGather:
    def __init__(self, place, own, out, sems, crossing):
        self.place, self.own, self.out, self.sems = place, own, out, sems
        self.crossing = crossing
        self.parts = [place.x, 1 - place.x] if crossing else [None]
        self.sent = []

    @staticmethod
    def semaphores(depth):
        sizes = (1, 1, 1, 4 * depth, 2 * depth, 2 * depth, 2 * depth, 4 * depth, 4 * depth)
        return [DMA((size,)) for size in sizes]

    def send(self, src, dst, send_sem, recv_sem, device, condition=None):
        copy = remote(src, dst, send_sem, recv_sem, device)
        guard(condition, copy.start)
        self.sent.append((copy, condition))

    def block(self, zi, y, c, part):
        if part is None:
            return self.out.at[zi, :, y, c]
        return self.out.at[zi, part, y, c]

    def slot(self, zi, part):
        return 2 * zi if part is None else 2 * zi + part

    def landed(self, ref, recv_sem, condition=None):
        guard(condition, remote(ref, ref, self.sems[3].at[0], recv_sem, self.place.flip_c()).wait_recv)

    def local(self):
        place = self.place
        source = self.own.at[place.x] if self.crossing else self.own
        return pltpu.make_async_copy(
            source, self.block(place.z, place.y, place.c, self.parts[0]), self.sems[0].at[0]
        )

    def begin(self):
        place = self.place
        self.send(
            self.own.at[1 - place.x],
            self.out.at[place.z, place.x, place.y, place.c],
            self.sems[1].at[0],
            self.sems[2].at[0],
            place.flip_x(),
        )
        self.spread(0, 0, place.z, None, place.x, self.own.at[place.x])

    def spread(self, k, side, zi, ok, part, source):
        place, depth = self.place, self.place.depth
        z_send, z_recv, y_send, y_recv, c_send, c_recv = self.sems[3:9]
        block, slot = self.block(zi, place.y, place.c, part), self.slot(zi, part)
        if k == 0 or side == 0:
            self.send(
                source,
                block,
                z_send.at[self.slot(k, part)],
                z_recv.at[slot],
                place.z_up(),
                both(place.up, ok),
            )
        if k == 0 or side == 1:
            self.send(
                source,
                block,
                z_send.at[2 * depth + self.slot(k, part)],
                z_recv.at[slot],
                place.z_down(),
                both(place.down, ok),
            )
        self.send(source, block, y_send.at[slot], y_recv.at[slot], place.flip_y(), ok)
        self.send(source, block, c_send.at[slot], c_recv.at[slot], place.flip_c(), ok)

    def arrive(self, k):
        place = self.place
        z_recv = self.sems[4]
        for side, (zi, ok) in enumerate(place.wave(k)):
            for number, part in enumerate(self.parts):
                block = self.block(zi, place.y, place.c, part)
                source = block
                if k > 0:
                    self.landed(block, z_recv.at[self.slot(zi, part)], ok)
                elif not self.crossing:
                    source = self.own
                elif number == 0:
                    continue
                else:
                    self.landed(block, self.sems[2].at[0])
                self.spread(k, side, zi, ok, part, source)

    def across(self, k):
        place, depth = self.place, self.place.depth
        y_recv, c_send, c_recv = self.sems[6:9]
        for zi, ok in place.wave(k):
            for part in self.parts:
                block = self.block(zi, 1 - place.y, place.c, part)
                self.landed(block, y_recv.at[self.slot(zi, part)], ok)
                slot = 2 * depth + self.slot(zi, part)
                self.send(block, block, c_send.at[slot], c_recv.at[slot], place.flip_c(), ok)

    def take(self, k):
        place, depth = self.place, self.place.depth
        c_recv = self.sems[8]
        for zi, ok in place.wave(k):
            for part in self.parts:
                slot = self.slot(zi, part)
                self.landed(self.block(zi, place.y, 1 - place.c, part), c_recv.at[slot], ok)
                slot = 2 * depth + slot
                self.landed(self.block(zi, 1 - place.y, 1 - place.c, part), c_recv.at[slot], ok)

    def settle(self):
        for copy, condition in self.sent:
            guard(condition, copy.wait_send)


class PairReduce:
    def __init__(self, place, own, out, buffers, sems, causal=False, crossing=False):
        self.place, self.own, self.out, self.sems = place, own, out, sems
        self.from_core, self.from_y, self.line, self.from_x = buffers
        self.causal, self.crossing = causal, crossing
        self.sent = []

    @staticmethod
    def scratch(depth, block):
        buffers = [
            pltpu.VMEM((depth, 2, 2) + block, BF16),
            pltpu.VMEM((depth, 2) + block, BF16),
            pltpu.VMEM((depth + 1, 2) + block, BF16),
            pltpu.VMEM((1,) + block, BF16),
        ]
        sems = [DMA((2 * depth,)), DMA((2 * depth,)), DMA((depth,)), DMA((depth,))]
        sems += [DMA((2 * depth,)), DMA((2 * depth,)), DMA((1,)), DMA((1,))]
        return buffers, sems

    def wave(self, k):
        waves = self.place.wave(k)
        return waves[:1] if self.causal else waves

    def send(self, src, dst, send_sem, recv_sem, device, condition=None):
        copy = remote(src, dst, send_sem, recv_sem, device)
        guard(condition, copy.start)
        self.sent.append((copy, condition))

    def landed(self, ref, recv_sem):
        remote(ref, ref, self.sems[0].at[0], recv_sem, self.place.flip_c()).wait_recv()

    def add(self, target, term):
        for x in range(2):
            add_into(target.at[x], term.at[x], target.shape[1])

    def cores(self, k):
        place = self.place
        for zi, ok in self.wave(k):
            for y in range(2):
                slot = 2 * zi + y
                self.send(
                    self.own.at[zi, :, y, 1 - place.c],
                    self.from_core.at[zi, y],
                    self.sems[0].at[slot],
                    self.sems[1].at[slot],
                    place.flip_c(),
                    ok,
                )

    def over(self, k):
        place = self.place
        for zi, ok in self.wave(k):

            def body(zi=zi):
                for y in (1 - place.y, place.y):
                    block = self.from_core.at[zi, y]
                    self.landed(block, self.sems[1].at[2 * zi + y])
                    self.add(block, self.own.at[zi, :, y, place.c])
                    if y is not place.y:
                        self.y_copy(zi).start()

            guard(ok, body)
            self.sent.append((self.y_copy(zi), ok))

    def y_copy(self, zi):
        place = self.place
        return remote(
            self.from_core.at[zi, 1 - place.y],
            self.from_y.at[zi],
            self.sems[2].at[zi],
            self.sems[3].at[zi],
            place.flip_y(),
        )

    def z_copy(self, k, side, zi):
        depth = self.place.depth
        direction = 1 - side
        slot = direction * depth + zi
        there = self.line.at[depth if k == 1 and direction == 1 else zi]
        to = self.place.z_up() if side == 1 else self.place.z_down()
        return remote(
            self.from_y.at[zi], there, self.sems[4].at[slot], self.sems[5].at[slot], to
        )

    def along(self, k):
        place, depth = self.place, self.place.depth
        for side, (zi, ok) in enumerate(self.wave(k)):
            block = self.from_y.at[zi]

            def body(zi=zi, side=side, block=block):
                self.landed(block, self.sems[3].at[zi])
                self.add(block, self.from_core.at[zi, place.y])

                def more(direction):
                    term = self.line.at[depth if k == 0 and direction == 1 else zi]
                    self.landed(term, self.sems[5].at[direction * depth + zi])
                    self.add(block, term)

                if k == 0:
                    if not self.causal:
                        pl.when(place.down)(functools.partial(more, 0))
                    pl.when(place.up)(functools.partial(more, 1))
                elif side == 0:
                    pl.when(place.up)(functools.partial(more, 1))
                else:
                    pl.when(place.down)(functools.partial(more, 0))
                if k > 0:
                    self.z_copy(k, side, zi).start()

            guard(ok, body)
            if k > 0:
                self.sent.append((self.z_copy(k, side, zi), ok))

    def swap(self):
        place = self.place
        self.send(
            self.from_y.at[place.z, 1 - place.x],
            self.from_x.at[0],
            self.sems[6].at[0],
            self.sems[7].at[0],
            place.flip_x(),
        )

    def finish(self):
        place = self.place
        if self.crossing:
            self.landed(self.from_x.at[0], self.sems[7].at[0])
            self.out[place.x] = self.from_y[place.z, place.x].astype(self.out.dtype)
            self.out[1 - place.x] = self.from_x[0].astype(self.out.dtype)
        else:
            self.out[...] = self.from_y[place.z].astype(self.out.dtype)

    def settle(self):
        for copy, condition in self.sent:
            guard(condition, copy.wait_send)


class Exchange:
    def __init__(self, place, own, out, sems):
        self.place, self.own, self.out, self.sems = place, own, out, sems
        self.count = 2 * place.depth
        self.sent = []
        self.y_f = place.f + 2 - 4 * place.y
        self.c_f = place.f + 1 - 2 * place.c
        self.yc_f = self.y_f + 1 - 2 * place.c

    @staticmethod
    def semaphores(depth):
        count = 2 * depth
        return [
            DMA((1,)),
            DMA((count,)),
            DMA((count,)),
            DMA((count,)),
            DMA((count,)),
            DMA((2 * count,)),
            DMA((2 * count,)),
        ]

    def send(self, block, send_sem, recv_sem, device, source=None):
        copy = remote(block if source is None else source, block, send_sem, recv_sem, device)
        copy.start()
        self.sent.append(copy)

    def block(self, offset, owner):
        origin = lax.rem(self.place.s + self.count - offset, self.count)
        return self.out.at[:, origin, owner]

    def landed(self, block, recv_sem):
        remote(block, block, self.sems[1].at[0], recv_sem, self.place.flip_c()).wait_recv()

    def local(self):
        return pltpu.make_async_copy(
            self.own.at[:, self.place.s], self.block(0, self.place.f), self.sems[0].at[0]
        )

    def depart(self, offset):
        place = self.place
        to = lax.rem(place.s + offset, self.count)
        self.send(
            self.block(0, place.f),
            self.sems[1].at[offset],
            self.sems[2].at[offset],
            (to, place.f),
            self.own.at[:, to],
        )

    def onward(self, offset):
        place = self.place
        block = self.block(offset, place.f)
        if offset > 0:
            self.landed(block, self.sems[2].at[offset])
        self.send(block, self.sems[3].at[offset], self.sems[4].at[offset], place.flip_y())
        slot = 2 * offset
        self.send(block, self.sems[5].at[slot], self.sems[6].at[slot], place.flip_c())

    def sideways(self, offset):
        block = self.block(offset, self.y_f)
        self.landed(block, self.sems[4].at[offset])
        slot = 2 * offset + 1
        self.send(block, self.sems[5].at[slot], self.sems[6].at[slot], self.place.flip_c())

    def last(self, offset):
        self.landed(self.block(offset, self.c_f), self.sems[6].at[2 * offset])
        self.landed(self.block(offset, self.yc_f), self.sems[6].at[2 * offset + 1])

    def settle(self):
        for copy in self.sent:
            copy.wait_send()


class Quarter:
    def __init__(self, place, own, out, sems):
        self.place, self.own, self.out, self.sems = place, own, out, sems
        self.sent = []

    @staticmethod
    def semaphores():
        return [DMA((1,)), DMA((3,)), DMA((3,))]

    def local(self):
        return pltpu.make_async_copy(self.own, self.out.at[self.place.f], self.sems[0].at[0])

    def send(self, source, block, slot, device):
        copy = remote(source, block, self.sems[1].at[slot], self.sems[2].at[slot], device)
        copy.start()
        self.sent.append(copy)

    def depart(self):
        place = self.place
        self.send(self.own, self.out.at[place.f], 0, place.flip_y())
        self.send(self.own, self.out.at[place.f], 1, place.flip_c())

    def landed(self, owner, slot):
        block = self.out.at[owner]
        remote(block, block, self.sems[1].at[0], self.sems[2].at[slot], self.place.flip_c()).wait_recv()

    def sideways(self):
        place = self.place
        y_f = place.f + 2 - 4 * place.y
        self.landed(y_f, 0)
        self.send(self.out.at[y_f], self.out.at[y_f], 2, place.flip_c())

    def last(self):
        place = self.place
        self.landed(place.f + 1 - 2 * place.c, 1)
        self.landed(place.f + 2 - 4 * place.y + 1 - 2 * place.c, 2)

    def settle(self):
        for copy in self.sent:
            copy.wait_send()


def stage(gather, step):
    depth = gather.place.depth
    if step < depth:
        gather.arrive(step)
    if 0 <= step - 1 < depth:
        gather.across(step - 1)
    if isinstance(gather, PairGather):
        if 0 <= step - 2 < depth:
            gather.take(step - 2)
        return
    if gather.wide and 0 <= step - 2 < depth:
        gather.hand(step - 2)
    if gather.wide and 0 <= step - 3 < depth:
        gather.take(step - 3)


def turned(vector, cosine, sine):
    return vector * cosine + pltpu.roll(vector, HEAD_DIM // 2, 1) * sine


HEAD_PLAN = (
    ("tables", "P0", "wide", "P1", "P2", "d1", "d5", "P3", "o0", "d7", "P4", "P5", "project", "K0", "o1", "c0", "n7"),
    ("K1", "K2", "d2", "K3", "K4", "o2", "d6", "c1", "K5", "n0", "A0", "d4", "A1", "o3", "A2"),
    ("o4", "s0", "n6", "A3", "s7", "o5", "mix", "n1", "n5", "d3", "o6", "D", "after", "h0", "keep", "h1"),
    ("c2", "s1", "n4", "n3", "s6", "s5", "h2", "n2", "c3", "S", "s3", "s4", "s2", "h3", "h4", "c4"),
)
HEAD_INS = 12
HEAD_OUTS = 16


def head_kernel(depth, *refs):
    (o_own, q_own, k_own, v_own, small_own, gate_own, up_own, down_own) = refs[:8]
    (tokens, cot, frequency, lengths) = refs[8:HEAD_INS]
    (
        pack_out,
        o_out,
        kv_out,
        cot_out,
        wide_out,
        down_out,
        hidden_out,
        queries_out,
        mixed_out,
        lse_out,
        middle_out,
        hidden_pair_out,
        mixed_low_out,
        pair_out,
        angles_out,
        begin,
    ) = refs[HEAD_INS : HEAD_INS + HEAD_OUTS]
    vectors = refs[HEAD_INS + HEAD_OUTS]
    rest = refs[HEAD_INS + HEAD_OUTS + 1 :]
    pack_all, o_all, kv_all, kv_own, hidden_two, lin, m_acc, l_acc, o_acc = rest[:9]
    pack, wide, down, mixed_pair, mixed_far, spread = rest[9:15]
    queries, mixed, lse, middle, hidden_pair, mixed_low, pair, angles = rest[15:23]
    sems = list(rest[23:])

    def take(count):
        taken = sems[:count]
        del sems[:count]
        return taken

    wide_need = len(Gather.semaphores(depth, True))
    line_need = len(Gather.semaphores(depth, False))
    count = 2 * depth
    devices = 4 * count
    rows, model = tokens.shape
    key_width = KV_HEADS * HEAD_DIM
    group_width = GROUP * HEAD_DIM
    qkv_width = group_width + 2 * HEAD_DIM

    place = Place(depth)
    for g in range(KV_HEADS):
        at = 0
        for source in (q_own, k_own, v_own):
            width = source.shape[1] // KV_HEADS
            pack[g, :, at : at + width] = source[:, g * width : (g + 1) * width]
            at += width
        pack[g, :, at:] = small_own[...]
    greet(place, [(lax.rem(place.s + offset, count), place.f) for offset in range(1, count)])
    pair_need = len(PairGather.semaphores(depth))
    g_pack = PairGather(place, pack, pack_all, take(pair_need), True)
    g_o = Gather(place, True, o_own, o_all, take(wide_need))
    g_kv = PairGather(place, kv_own, kv_all, take(pair_need), False)
    g_cot = Gather(place, False, cot, cot_out, take(line_need + 2), True)
    g_hidden = Gather(place, False, hidden_two, hidden_out, take(line_need))
    x_wide = Exchange(place, wide, wide_out, take(len(Exchange.semaphores(depth))))
    x_down = Quarter(place, down, down_out, take(len(Quarter.semaphores())))
    out_sem, x_send, x_recv = take(3)

    g_pack.begin()
    token_copy = remote(
        tokens, pair.at[place.x], x_send.at[0], x_recv.at[0], place.flip_x()
    )
    token_copy.start()
    pair[place.x] = tokens[...]
    pack_local = g_pack.local()
    pack_local.start()
    pack_local.wait()
    few = down_own.shape[0]
    filled = down.shape[0]
    locals_ = [job.local() for job in (g_o, g_cot, x_wide, x_down)]
    for copy in locals_[:2]:
        copy.start()
    inputs = tokens[...].astype(F32)

    def pack_wide():
        for side, source in enumerate((gate_own, up_own)):
            for to in range(count):
                parts = []
                for owner in range(4):
                    low = (4 * to + owner) * few
                    parts.append(source[:, low : low + few])
                    parts.append(jnp.zeros((wide.shape[2], filled - few), BF16))
                wide[side, to] = jnp.concatenate(parts, axis=1)
        locals_[2].start()

    def tables():
        down[...] = jnp.concatenate(
            [down_own[...], jnp.zeros((filled - few, model), BF16)], axis=0
        )
        locals_[3].start()
        ahead = lax.broadcasted_iota(jnp.int32, (1, HEAD_DIM), 1) < HEAD_DIM // 2
        for x in range(2):
            first_row = ((2 * place.z + x) * 4 + place.f) * rows
            positions = first_row + lax.broadcasted_iota(jnp.int32, (rows, 1), 0)
            start, found = jnp.int32(0), jnp.zeros((rows, 1), jnp.int32)
            for number in range(lengths.shape[0]):
                found = jnp.where(positions >= start, start, found)
                start = start + lengths[number]
            begin[x] = found
            turns = (positions - found).astype(F32) * frequency[...]
            angles[x, 0] = jnp.cos(turns)
            sine = jnp.sin(turns)
            angles[x, 1] = jnp.where(ahead, -sine, sine)

    part = model // depth
    own_head = pl.ds(pl.multiple_of(place.x * HEAD_DIM, HEAD_DIM), HEAD_DIM)
    own_heads = pl.ds(pl.multiple_of(place.x * group_width, group_width), group_width)
    kv_local = g_kv.local()
    hidden_local = g_hidden.local()
    mixed_copy = remote(
        mixed_pair.at[1 - place.x], mixed_far, x_send.at[1], x_recv.at[1], place.flip_x()
    )

    def project():
        share = key_width // devices
        chosen = lax.broadcasted_iota(jnp.int32, (model, key_width), 1)
        chosen = lax.div(chosen, share) * (model // devices) + lax.rem(chosen, share)
        chosen = lax.broadcasted_iota(jnp.int32, (model, key_width), 0) == chosen
        small = pack_all[:, :, :, :, :, qkv_width:].reshape(model, 128).astype(F32).T
        vectors[...] = small[:8]
        spread[...] = jnp.dot(
            small[:8].astype(BF16), chosen.astype(BF16), preferred_element_type=F32
        )
        for copy in locals_:
            copy.wait()
        token_copy.wait_recv()
        pair_inputs = pair[...].reshape(2 * rows, model).astype(F32)
        inv_pair = lax.rsqrt(jnp.mean(pair_inputs * pair_inputs, axis=-1, keepdims=True) + EPSILON)
        hidden_pair[...] = (pair_inputs * inv_pair * small[0:1]).astype(BF16)
        for zi in range(depth):
            weights = pack_all[zi][:, :, :, :, :qkv_width].reshape(part, qkv_width)
            term = jnp.dot(
                hidden_pair[:, zi * part : (zi + 1) * part], weights, preferred_element_type=F32
            )
            if zi == 0:
                lin[...] = term
            else:
                lin[...] += term
        for x in range(2):
            at = slice(x * rows, (x + 1) * rows)
            head = lin[at, group_width : group_width + HEAD_DIM] + spread[2:3, own_head]
            kv_own[x, :, :HEAD_DIM] = turned(head, angles[x, 0], angles[x, 1]).astype(BF16)
            values = lin[at, group_width + HEAD_DIM :] + spread[3:4, own_head]
            kv_own[x, :, HEAD_DIM:] = values.astype(BF16)
        kv_local.start()

    def queries_of():
        query_bias = vectors[1:2, own_heads]
        for x in range(2):
            for j in range(GROUP):
                lanes = slice(j * HEAD_DIM, (j + 1) * HEAD_DIM)
                head = lin[x * rows : (x + 1) * rows, lanes] + query_bias[:, lanes]
                queries[x, j * rows : (j + 1) * rows, :] = turned(
                    head, angles[x, 0], angles[x, 1]
                ).astype(BF16)
        kv_local.wait()

    span = 4 * rows
    scale = HEAD_DIM ** (-0.5) * LOG2E
    m_acc[...] = jnp.full_like(m_acc, -1e30)
    l_acc[...] = jnp.zeros_like(l_acc)
    o_acc[...] = jnp.zeros_like(o_acc)
    local_rows = lax.broadcasted_iota(jnp.int32, (rows, span), 0)
    offsets = lax.broadcasted_iota(jnp.int32, (rows, span), 1)

    def attend(number, carry):
        keys_at = number * span + offsets
        block = kv_all.at[lax.div(number, 2), lax.rem(number, 2)]
        key = block[:, :, :, :HEAD_DIM].reshape(span, HEAD_DIM)
        value = block[:, :, :, HEAD_DIM:].reshape(span, HEAD_DIM)
        for x in range(2):
            places = ((2 * place.z + x) * 4 + place.f) * rows + local_rows
            visible = jnp.logical_and(keys_at >= begin[x], keys_at <= places)
            scores = mul_t(queries[x], key)
            scores = scores.reshape(GROUP, rows, span) * scale
            scores = jnp.where(visible[None], scores, -1e30).reshape(GROUP * rows, span)
            old = m_acc[x]
            new = jnp.maximum(old, jnp.max(scores, axis=-1, keepdims=True))
            weights = jnp.exp2(scores - new[:, :1])
            fade = jnp.exp2(old - new)
            l_acc[x] = l_acc[x] * fade + jnp.sum(weights, axis=-1, keepdims=True)
            o_acc[x] = o_acc[x] * fade + jnp.dot(
                weights.astype(BF16), value, preferred_element_type=F32
            )
            m_acc[x] = new
        return carry

    def attend_quarter(piece):
        low, high = piece * count // 4, (piece + 1) * count // 4
        reach = 2 * place.z + 2
        lax.fori_loop(jnp.minimum(low, reach), jnp.minimum(high, reach), attend, 0)

    def mix():
        for x in range(2):
            total = o_acc[x] / l_acc[x]
            mixed[x] = total
            lse[x] = m_acc[x] + jnp.log2(l_acc[x])
            mixed_pair[x] = total.astype(BF16)
        mixed_copy.start()

    def after_attention():
        mixed_copy.wait_recv()
        for j in range(GROUP):
            at = slice(j * rows, (j + 1) * rows)
            near = pl.multiple_of((place.x * GROUP + j) * HEAD_DIM, HEAD_DIM)
            far = pl.multiple_of(((1 - place.x) * GROUP + j) * HEAD_DIM, HEAD_DIM)
            mixed_low[:, pl.ds(near, HEAD_DIM)] = mixed_pair[place.x, at, :]
            mixed_low[:, pl.ds(far, HEAD_DIM)] = mixed_far[at, :]
        after = inputs
        for zi in range(depth):
            after = after + jnp.dot(
                mixed_low[:, zi * part : (zi + 1) * part],
                o_all[zi].reshape(part, model),
                preferred_element_type=F32,
            )
        middle[...] = after
        inv_two = lax.rsqrt(jnp.mean(after * after, axis=-1, keepdims=True) + EPSILON)
        hidden_two[...] = (after * inv_two * vectors[4:5]).astype(BF16)
        hidden_local.start()

    keeps = [
        pltpu.make_async_copy(source, target, out_sem.at[number])
        for number, (source, target) in enumerate(
            (
                (pack_all, pack_out),
                (o_all, o_out),
                (kv_all, kv_out),
                (queries, queries_out),
                (mixed, mixed_out),
                (lse, lse_out),
                (middle, middle_out),
                (hidden_pair, hidden_pair_out),
                (mixed_low, mixed_low_out),
                (pair, pair_out),
                (angles, angles_out),
            )
        )
    ]

    def keep():
        for copy in keeps:
            copy.start()

    jobs = {"P": g_pack, "K": g_kv, "o": g_o, "c": g_cot, "h": g_hidden}
    moves = {"d": x_wide.depart, "n": x_wide.onward, "s": x_wide.sideways, "A": attend_quarter}
    works = {
        "wide": pack_wide,
        "tables": tables,
        "project": project,
        "mix": mix,
        "after": after_attention,
        "keep": keep,
        "D": x_down.depart,
        "S": x_down.sideways,
    }
    for words in HEAD_PLAN:
        for word in words:
            if word in works:
                works[word]()
            elif word[0] in moves:
                moves[word[0]](int(word[1:]))
            else:
                stage(jobs[word[0]], int(word[1:]))
                if word == "K0":
                    queries_of()

    hidden_local.wait()
    for offset in range(count):
        x_wide.last(offset)
    x_down.last()
    for copy in keeps:
        copy.wait()
    token_copy.wait_send()
    mixed_copy.wait_send()
    for job in (g_pack, g_o, g_kv, g_cot, g_hidden, x_wide, x_down):
        job.settle()


def call_head(depth, collective_id, hbm, vmems, lengths):
    (o_own,) = hbm
    q_own, k_own, v_own, small_own, gate_own, _, down_own, tokens, cot = vmems[:9]
    count = 2 * depth
    few = down_own.shape[0]
    filled = -(-few // 16) * 16
    qkv_width = (GROUP + 2) * HEAD_DIM
    width = qkv_width + small_own.shape[1]
    pack = jax.ShapeDtypeStruct((q_own.shape[0], width), BF16)
    wide = jax.ShapeDtypeStruct((2, count, gate_own.shape[0], 4 * filled), BF16)
    down = jax.ShapeDtypeStruct((filled, down_own.shape[1]), BF16)
    rows, model = tokens.shape
    key_width = KV_HEADS * HEAD_DIM
    stacked = GROUP * rows
    kv_own = jax.ShapeDtypeStruct((rows, 2 * HEAD_DIM), BF16)
    any_, vmem = pl.BlockSpec(memory_space=pl.ANY), pl.BlockSpec(memory_space=pltpu.VMEM)
    heads = (KV_HEADS, stacked, HEAD_DIM)
    outs = [
        gather_shape(depth, True, pack),
        gather_shape(depth, True, o_own),
        gather_shape(depth, True, kv_own),
        gather_shape(depth, False, cot),
        jax.ShapeDtypeStruct((2, count, 4) + wide.shape[2:], BF16),
        jax.ShapeDtypeStruct((4,) + down.shape, BF16),
        gather_shape(depth, False, tokens),
        jax.ShapeDtypeStruct(heads, BF16),
        jax.ShapeDtypeStruct(heads, F32),
        jax.ShapeDtypeStruct(heads, F32),
        jax.ShapeDtypeStruct((rows, model), F32),
        jax.ShapeDtypeStruct((2 * rows, model), BF16),
        jax.ShapeDtypeStruct((rows, model), BF16),
        jax.ShapeDtypeStruct((2, rows, model), BF16),
        jax.ShapeDtypeStruct((2, 2, rows, HEAD_DIM), F32),
        jax.ShapeDtypeStruct((2, rows, 1), jnp.int32),
        jax.ShapeDtypeStruct((8, model), F32),
    ]
    scratch = [pltpu.VMEM(out.shape, BF16) for out in outs[:3]]
    scratch += [
        pltpu.VMEM((2,) + kv_own.shape, BF16),
        pltpu.VMEM((rows, model), BF16),
        pltpu.VMEM((2 * rows, qkv_width), F32),
        pltpu.VMEM(heads, F32),
        pltpu.VMEM(heads, F32),
        pltpu.VMEM(heads, F32),
        pltpu.VMEM((KV_HEADS,) + pack.shape, BF16),
        pltpu.VMEM(wide.shape, BF16),
        pltpu.VMEM(down.shape, BF16),
        pltpu.VMEM(heads, BF16),
        pltpu.VMEM(heads[1:], BF16),
        pltpu.VMEM((8, key_width), F32),
    ]
    scratch += [pltpu.VMEM(out.shape, out.dtype) for out in outs[7:15]]
    scratch += PairGather.semaphores(depth) + Gather.semaphores(depth, True)
    scratch += PairGather.semaphores(depth)
    scratch += Gather.semaphores(depth, False, True) + Gather.semaphores(depth, False)
    scratch += Exchange.semaphores(depth) + Quarter.semaphores()
    scratch += [DMA((11,)), DMA((2,)), DMA((2,))]
    return pl.pallas_call(
        functools.partial(head_kernel, depth),
        out_shape=outs,
        in_specs=[any_] + [vmem] * len(vmems) + [pl.BlockSpec(memory_space=pltpu.SMEM)],
        out_specs=[any_] * 15 + [vmem] * 2,
        scratch_shapes=scratch,
        compiler_params=pltpu.CompilerParams(
            collective_id=collective_id, has_side_effects=True, vmem_limit_bytes=VMEM_LIMIT
        ),
    )(*hbm, *vmems, lengths)


def t_mul(left, right):
    return lax.dot_general(left, right, (((0,), (0,)), ((), ())), preferred_element_type=F32)


def mul_t(left, right):
    return lax.dot_general(left, right, (((1,), (1,)), ((), ())), preferred_element_type=F32)


CUTS = ((0, 512), (512, 1024), (1024, 1152))


def middle_kernel(depth, *refs):
    (hidden_all, cot_all, wide_all, down_all, o_own) = refs[:5]
    (middle, cotangent, vectors) = refs[5:8]
    (layer_out, d_middle, d_mixed, d_branch, gain_two, down_out, wide_out) = refs[8:15]
    (tokens_v, grads_v, w_part, d_part, act, d_both, dh_part, out_part) = refs[15:23]
    (dh_sum, out_sum, w_core, w_y, d_core, o_all) = refs[23:29]
    rest = list(refs[29:])

    def take(count):
        taken = rest[:count]
        del rest[:count]
        return taken

    count = 2 * depth
    rows, model = middle.shape
    units = act.shape[2]
    part = model // depth
    buffers, sems = Reduce.scratch(depth, False, (rows, model))
    place = Place(depth)
    r_dh = Reduce(place, False, rows, dh_part, dh_sum, take(len(buffers)), take(len(sems)))
    r_out = Reduce(place, False, rows, out_part, out_sum, take(len(buffers)), take(len(sems)))
    load_sem, wc_send, wc_recv, wy_send, wy_recv, dc_send, dc_recv = take(7)
    sent = []

    def send(src, dst, send_sem, recv_sem, device):
        copy = remote(src, dst, send_sem, recv_sem, device)
        copy.start()
        sent.append(copy)

    def landed(ref, recv_sem):
        remote(ref, ref, wc_send.at[0], recv_sem, place.flip_c()).wait_recv()

    loads = [
        pltpu.make_async_copy(source, target, load_sem.at[number])
        for number, (source, target) in enumerate(
            (
                (hidden_all, tokens_v),
                (wide_all, w_part),
                (cot_all, grads_v),
                (down_all, d_part),
            )
        )
    ]
    for copy in loads:
        copy.start()
    greet(place)
    mine_y, other_y = place.y, 1 - place.y
    wide_rows = w_part.shape[-2]
    half = lax.div(place.z, 2)
    tiles = [3 - 3 * half, 2 - half, 1 + 4 * half - place.z, place.z]
    for copy in loads:
        copy.wait()

    def weights(side, low, high):
        return w_part[side, :, :, :, :, low:high].reshape(model, high - low)

    def forward(zi):
        tokens = tokens_v[zi].reshape(2 * rows, model)
        grads = grads_v[zi].reshape(2 * rows, model)
        out = None
        for low, high in CUTS:
            gate = jnp.dot(tokens, weights(0, low, high), preferred_element_type=F32)
            up = jnp.dot(tokens, weights(1, low, high), preferred_element_type=F32)
            d_act = mul_t(grads, d_part[low:high, :])
            sigma = jax.nn.sigmoid(gate)
            silu = gate * sigma
            act[zi, :, low:high] = (silu * up).astype(BF16)
            d_both[zi, :, low:high] = (
                d_act * up * sigma * (1.0 + gate * (1.0 - sigma))
            ).astype(BF16)
            d_both[zi, :, units + low : units + high] = (d_act * silu).astype(BF16)
        total = mul_t(d_both[zi, :, :units], weights(0, 0, units))
        total = total + mul_t(d_both[zi, :, units:], weights(1, 0, units))
        dh_part[zi] = total.astype(BF16).reshape(2, rows, model)
        out = jnp.dot(act[zi], d_part[...], preferred_element_type=F32)
        out_part[zi] = out.astype(BF16).reshape(2, rows, model)

    def tile(number, carry):
        zi = jnp.where(
            number == 0,
            tiles[0],
            jnp.where(number == 1, tiles[1], jnp.where(number == 2, tiles[2], tiles[3])),
        )
        forward(zi)
        r_dh.cross(zi)
        return carry

    lax.fori_loop(0, depth, tile, 0)
    for zi in tiles:
        r_out.cross(zi)
    r_dh.crossed()
    r_out.crossed()

    def wide_chunk(k, carry):
        lanes = pl.ds(pl.multiple_of(k * part, part), part)
        tokens = tokens_v[:, :, :, lanes].reshape(count * rows, part)
        term = t_mul(tokens, d_both[...].reshape(count * rows, 2 * units))
        for side in range(2):
            w_part[side, pl.ds(2 * k, 2)] = (
                term[:, side * units : (side + 1) * units]
                .astype(BF16)
                .reshape(2, 2, 2, wide_rows, units)
            )
        for step in range(2):
            to = 2 * k + step
            for y in range(2):
                remote(
                    w_part.at[:, to, y, 1 - place.c],
                    w_core.at[y, to],
                    wc_send.at[2 * to + y],
                    wc_recv.at[2 * to + y],
                    place.flip_c(),
                ).start()
        return carry

    def wide_cores(to):
        for y in (other_y, mine_y):
            landed(w_core.at[y, to], wc_recv.at[2 * to + y])
            for side in range(2):
                add_into(
                    w_core.at[y, to, side], w_part.at[side, to, y, place.c], wide_rows
                )
            if y is other_y:
                remote(
                    w_core.at[y, to], w_y.at[to], wy_send.at[to], wy_recv.at[to], place.flip_y()
                ).start()

    def wide_across(to, carry):
        landed(w_y.at[to], wy_recv.at[to])
        for side in range(2):
            add_into(w_y.at[to, side], w_core.at[mine_y, to, side], wide_rows)
        pltpu.make_async_copy(w_y.at[to], wide_out.at[to], load_sem.at[to]).start()
        return carry

    def wide_step(k, carry):
        wide_chunk(k, 0)
        pl.when(k > 0)(lambda: wide_cores(2 * k - 2))
        pl.when(k > 0)(lambda: wide_cores(2 * k - 1))
        return carry

    order = list(range(depth - 1, -1, -1))
    lax.fori_loop(0, depth - 2, wide_step, 0)
    r_dh.along(order[0])
    r_dh.along(order[1])
    lax.fori_loop(depth - 2, depth, wide_step, 0)
    wide_cores(count - 2)
    wide_cores(count - 1)
    r_dh.along(order[2])
    pieces = [
        pltpu.make_async_copy(o_own.at[zi], o_all.at[zi % 2], load_sem.at[zi])
        for zi in range(depth)
    ]
    for copy in pieces[:2]:
        copy.start()

    def down_chunk(k, carry):
        lanes = pl.ds(pl.multiple_of(k * 384, 384), 384)
        chunk = act[:, :, lanes].reshape(count * rows, 384)
        d_part[lanes, :] = t_mul(chunk, grads_v[...].reshape(count * rows, model)).astype(BF16)
        return carry

    lax.fori_loop(0, units // 384, down_chunk, 0)
    down_rows = units // 4

    def down_block(owner):
        return d_part.at[pl.ds(pl.multiple_of(owner * down_rows, down_rows), down_rows)]

    for y in (other_y, mine_y):
        send(
            down_block(2 * y + 1 - place.c),
            d_core.at[y],
            dc_send.at[y],
            dc_recv.at[y],
            place.flip_c(),
        )
    r_dh.along(order[3])
    r_dh.finish()

    after = middle[...]
    inv_two = lax.rsqrt(jnp.mean(after * after, axis=-1, keepdims=True) + EPSILON)
    normed = after * inv_two
    d_hidden = dh_sum[...]
    gain_two[...] = jnp.broadcast_to(
        jnp.sum(d_hidden * normed, axis=0, keepdims=True), gain_two.shape
    )
    scaled = d_hidden * vectors[4:5]
    total = cotangent[...].astype(F32) + inv_two * (
        scaled - normed * jnp.mean(scaled * normed, axis=-1, keepdims=True)
    )
    d_middle[...] = total
    d_branch[...] = total.astype(BF16)
    for zi in range(depth):
        pieces[zi].wait()
        term = mul_t(d_branch[...], o_all[zi % 2].reshape(part, model)).astype(BF16)
        for piece in range(part // HEAD_DIM):
            h = zi * (part // HEAD_DIM) + piece
            at = (h % GROUP) * rows
            d_mixed[h // GROUP, at : at + rows, :] = term[
                :, piece * HEAD_DIM : (piece + 1) * HEAD_DIM
            ]
        if zi + 2 < depth:
            pieces[zi + 2].start()
    for y in (other_y, mine_y):
        landed(d_core.at[y], dc_recv.at[y])
        add_into(d_core.at[y], down_block(2 * y + place.c), down_rows)
    keep = pltpu.make_async_copy(d_core, down_out, load_sem.at[count])
    keep.start()
    for step in range(depth):
        r_out.along(order[step])
        lax.fori_loop(2 * step, 2 * step + 2, wide_across, 0)
    r_out.finish()
    layer_out[...] = (middle[...] + out_sum[...]).astype(BF16)
    keep.wait()

    def end(to, carry):
        pltpu.make_async_copy(w_y.at[to], wide_out.at[to], load_sem.at[to]).wait()
        for y in range(2):
            slot = 2 * to + y
            remote(
                w_core.at[y, to], w_core.at[y, to], wc_send.at[slot], wc_recv.at[slot], place.flip_c()
            ).wait_send()
        remote(
            w_y.at[to], w_y.at[to], wy_send.at[to], wy_recv.at[to], place.flip_y()
        ).wait_send()
        return carry

    lax.fori_loop(0, count, end, 0)
    r_dh.settle()
    r_out.settle()
    for copy in sent:
        copy.wait_send()


def call_middle(depth, collective_id, hbm, vmems):
    hidden, cot, wide, down, o_all = hbm
    count = 2 * depth
    rows, model = vmems[0].shape
    units, wide_rows = wide.shape[-1], wide.shape[-2]
    any_, vmem = pl.BlockSpec(memory_space=pl.ANY), pl.BlockSpec(memory_space=pltpu.VMEM)
    buffers, sems = Reduce.scratch(depth, False, (rows, model))
    scratch = [pltpu.VMEM((depth, 2, rows, model), BF16)] * 2
    scratch += [pltpu.VMEM(wide.shape, BF16), pltpu.VMEM(down.shape, BF16)]
    scratch += [pltpu.VMEM((depth, 2 * rows, width), BF16) for width in (units, 2 * units)]
    scratch += [pltpu.VMEM((depth, 2, rows, model), BF16)] * 2
    scratch += [pltpu.VMEM((rows, model), F32)] * 2
    scratch += [
        pltpu.VMEM((2, count, 2, wide_rows, units), BF16),
        pltpu.VMEM((count, 2, wide_rows, units), BF16),
        pltpu.VMEM((2, units // 4, model), BF16),
        pltpu.VMEM((2,) + o_all.shape[1:], BF16),
    ]
    scratch += buffers + sems + buffers + sems
    scratch += [DMA((count + 1,)), DMA((2 * count,)), DMA((2 * count,))]
    scratch += [DMA((count,)), DMA((count,)), DMA((2,)), DMA((2,))]
    return pl.pallas_call(
        functools.partial(middle_kernel, depth),
        out_shape=[
            jax.ShapeDtypeStruct((rows, model), BF16),
            jax.ShapeDtypeStruct((rows, model), F32),
            jax.ShapeDtypeStruct((KV_HEADS, GROUP * rows, HEAD_DIM), BF16),
            jax.ShapeDtypeStruct((rows, model), BF16),
            jax.ShapeDtypeStruct((8, model), F32),
            jax.ShapeDtypeStruct((2, units // 4, model), BF16),
            jax.ShapeDtypeStruct((count, 2, wide_rows, units), BF16),
        ],
        in_specs=[any_] * 5 + [vmem] * 3,
        out_specs=[vmem] * 5 + [any_] * 2,
        scratch_shapes=scratch,
        compiler_params=pltpu.CompilerParams(
            collective_id=collective_id, has_side_effects=True, vmem_limit_bytes=VMEM_JOINED
        ),
    )(*hbm, *vmems)


LAST_PLAN = (
    ("d7", "d4", "d2", "d3", "down", "delta", "a0", "a1", "out"),
    ("Ck1", "Ck0", "Yk1", "d5", "Co0", "d1", "Co2", "Bo0", "a2"),
    ("Ck2", "Yk0", "a3", "Bo2", "Zk0", "Ck3", "turn", "Yk3", "Yk2"),
    ("Co1", "Zk1", "Co3", "hq", "Bo1", "query", "Zk2", "Bo3", "Cq0"),
    ("Cq2", "Ao0", "Cq1", "Zk3", "key", "Ao1", "Ao2", "d6", "hk"),
    ("kg", "small", "Cs0", "Yq0", "Cs2", "Cs1", "Zo0", "Yq1", "Ys0"),
    ("Cq3", "Ys2", "Yq2", "Zo1", "Cs3", "Zq0", "Ys1", "Ys3", "Zo2"),
    ("Yq3", "Ao3", "input", "Zs0", "Zq1", "Zs1", "Zq2", "Zs2", "Zq3"),
    ("Xq", "Zs3", "Xs", "Zo3"),
)


def follow_last(plan, works, depart, attend_wave, jobs):
    depth = 4
    steps = {"C": "cores", "B": "over_second", "A": "over_first", "Z": "along", "Y": "over"}
    for words in plan:
        for word in words:
            if word in works:
                works[word]()
            elif word[0] == "d":
                depart(int(word[1:]))
            elif word[0] == "a":
                attend_wave(int(word[1:]))
            else:
                getattr(jobs[word[1]], steps[word[0]])(depth - 1 - int(word[2:]))


def last_kernel(depth, *refs):
    (kv_own, pack_own, wide, down) = refs[:4]
    (d_mixed, angles, begin, vectors, gain_two) = refs[4:9]
    late_own = refs[9:17]
    (input_grad, q_out, kvs_out, o_out, down_out, wide_out) = refs[17:23]
    (kv_all, weights, d_query, delta, d_lin, d_keys, d_kv) = refs[23:30]
    (o_part, q_part, kvs_part) = refs[30:33]
    (d_near, d_far, d_hidden, kv_weights, d_pair, h_send, h_far, lines, pairs) = refs[33:42]
    late = refs[42:50]
    queries, mixed, lse, mixed_low, d_branch, hidden_pair, pair, d_middle = late
    rest = list(refs[50:])

    def take(number):
        taken = rest[:number]
        del rest[:number]
        return taken

    count = 2 * depth
    devices = 4 * count
    _, rows, model = pair.shape
    part = model // depth
    key_width = KV_HEADS * HEAD_DIM
    group_width = GROUP * HEAD_DIM
    qkv_width = group_width + 2 * HEAD_DIM
    model_rows = model // devices
    share = key_width // devices
    span = 4 * rows
    score_scale = HEAD_DIM ** (-0.5)
    scale = score_scale * LOG2E

    place = Place(depth)
    buffers, sems = Reduce.scratch(depth, True, o_part.shape[-2:])
    r_o = Reduce(
        place, True, model_rows, o_part, o_out, take(len(buffers)), take(len(sems))
    )

    def reduce_of(own, out, causal=False, crossing=True):
        buffers, sems = PairReduce.scratch(depth, own.shape[-2:])
        return PairReduce(
            place, own, out, take(len(buffers)), take(len(sems)), causal, crossing
        )

    r_kv = reduce_of(d_keys, d_kv, True, False)
    r_q = reduce_of(q_part, q_out)
    r_s = reduce_of(kvs_part, kvs_out)
    load_sem, e_send, e_recv, y_send, y_recv, x_send, x_recv, late_sem = take(8)
    order = list(range(depth - 1, -1, -1))
    sent = []

    def depart(offset):
        to = lax.rem(place.s + offset, count)
        copy = remote(
            wide.at[to], wide_out.at[place.s], e_send.at[offset], e_recv.at[offset], (to, place.f)
        )
        copy.start()
        sent.append(copy)

    kv_load = pltpu.make_async_copy(kv_own, kv_all, load_sem.at[0])
    kv_load.start()
    late_loads = [
        pltpu.make_async_copy(source, target, late_sem.at[number])
        for number, (source, target) in enumerate(zip(late_own, late))
    ]
    for copy in late_loads:
        copy.start()
    own_wide = pltpu.make_async_copy(wide.at[place.s], wide_out.at[place.s], load_sem.at[1])
    own_wide.start()
    down_load = pltpu.make_async_copy(down.at[place.y], d_near, load_sem.at[2 + depth])
    down_load.start()
    greet(place, [(lax.rem(place.s + offset, count), place.f) for offset in range(1, count)])
    mixed_copy = remote(
        d_mixed.at[1 - place.x],
        d_pair.at[place.x],
        x_send.at[0],
        x_recv.at[0],
        place.flip_x(),
    )
    mixed_copy.start()
    sent.append(mixed_copy)
    d_pair[place.x] = d_mixed[place.x]
    down_copy = remote(
        down.at[1 - place.y], d_far, y_send.at[0], y_recv.at[0], place.flip_y()
    )
    hidden_copy = remote(h_send, h_far, x_send.at[1], x_recv.at[1], place.flip_x())
    loads = [
        pltpu.make_async_copy(pack_own.at[zi], weights.at[zi % 2], load_sem.at[2 + zi])
        for zi in range(depth)
    ]

    local_rows = lax.broadcasted_iota(jnp.int32, (rows, span), 0)
    offsets = lax.broadcasted_iota(jnp.int32, (rows, span), 1)

    def attend(number, carry):
        keys_at = number * span + offsets
        z, x_at = lax.div(number, 2), lax.rem(number, 2)
        block = kv_all.at[z, x_at]
        key = block[:, :, :, :HEAD_DIM].reshape(span, HEAD_DIM)
        value = block[:, :, :, HEAD_DIM:].reshape(span, HEAD_DIM)
        d_key, d_value = None, None
        for x in range(2):
            places = ((2 * place.z + x) * 4 + place.f) * rows + local_rows
            visible = jnp.logical_and(keys_at >= begin[x], keys_at <= places)
            scores = mul_t(queries[x], key)
            d_probs = mul_t(d_pair[x], value)
            probs = jnp.exp2(scores * scale - lse[x][:, :1])
            probs = jnp.where(
                visible[None], probs.reshape(GROUP, rows, span), 0.0
            ).reshape(GROUP * rows, span)
            d_scores = (probs * (d_probs - delta[x][:, :1])).astype(BF16)
            d_query[x] += jnp.dot(d_scores, key, preferred_element_type=F32)
            key_term = t_mul(d_scores, queries[x])
            value_term = t_mul(probs.astype(BF16), d_pair[x])
            d_key = key_term if x == 0 else d_key + key_term
            d_value = value_term if x == 0 else d_value + value_term
        target = d_keys.at[z, x_at]
        target[:, :, :, :HEAD_DIM] = d_key.astype(BF16).reshape(2, 2, rows, HEAD_DIM)
        target[:, :, :, HEAD_DIM:] = d_value.astype(BF16).reshape(2, 2, rows, HEAD_DIM)
        return carry

    def normed_of(rows_of):
        inputs = rows_of.astype(F32)
        inverse = lax.rsqrt(jnp.mean(inputs * inputs, axis=-1, keepdims=True) + EPSILON)
        return inputs * inverse, inverse

    def out_gradient():
        for copy in late_loads[3:5]:
            copy.wait()
        for copy in loads[:2]:
            copy.start()
        for zi in range(depth):
            lanes = slice(zi * part, (zi + 1) * part)
            term = t_mul(mixed_low[:, lanes], d_branch[...]).astype(BF16)
            o_part[zi] = term.reshape(2, 2, 2, model_rows, model)

    def deltas():
        mixed_copy.wait_recv()
        for copy in late_loads[:3]:
            copy.wait()
        for x in range(2):
            delta[x] = jnp.broadcast_to(
                jnp.sum(d_pair[x].astype(F32) * mixed[x], axis=-1, keepdims=True),
                delta.shape[1:],
            )
        d_query[...] = jnp.zeros_like(d_query)
        kv_load.wait()

    def attend_wave(step):
        zi = place.z - order[step]
        low = jnp.maximum(2 * zi, 0)
        high = jnp.maximum(2 * zi + 2, 0)
        lax.fori_loop(low, high, attend, 0)

    def query_turn():
        for x in range(2):
            for j in range(GROUP):
                lanes = slice(j * HEAD_DIM, (j + 1) * HEAD_DIM)
                head = d_query[x, j * rows : (j + 1) * rows, :] * score_scale
                d_lin[x * rows : (x + 1) * rows, lanes] = turned(
                    head, angles[x, 0], -angles[x, 1]
                ).astype(BF16)

    def query_gradient():
        late_loads[5].wait()
        for zi in range(depth):
            lanes = slice(zi * part, (zi + 1) * part)
            term = t_mul(hidden_pair[:, lanes], d_lin[:, :group_width]).astype(BF16)
            q_part[zi] = term.reshape(2, 2, 2, model_rows, group_width)

    def key_turn():
        r_kv.finish()
        for x in range(2):
            at = slice(x * rows, (x + 1) * rows)
            head = d_kv[x, :, :HEAD_DIM] * score_scale
            d_lin[at, group_width : group_width + HEAD_DIM] = turned(
                head, angles[x, 0], -angles[x, 1]
            ).astype(BF16)
            d_lin[at, group_width + HEAD_DIM :] = d_kv[x, :, HEAD_DIM:].astype(BF16)

    def hidden_query():
        for zi in range(depth):
            lanes = slice(zi * part, (zi + 1) * part)
            loads[zi].wait()
            block = weights[zi % 2][:, :, :, :, :group_width].reshape(part, group_width)
            term = mul_t(d_lin[:, :group_width], block)
            for x in range(2):
                d_hidden[x, :, lanes] = term[x * rows : (x + 1) * rows]
            block = weights[zi % 2][:, :, :, :, group_width:qkv_width]
            kv_weights[lanes, :] = block.reshape(part, 2 * HEAD_DIM)
            if zi + 2 < depth:
                loads[zi + 2].start()

    def hidden_key():
        for zi in range(depth):
            lanes = slice(zi * part, (zi + 1) * part)
            term = mul_t(d_lin[:, group_width:], kv_weights[lanes, :])
            for x in range(2):
                d_hidden[x, :, lanes] += term[x * rows : (x + 1) * rows]
        h_send[...] = d_hidden[1 - place.x].astype(BF16)
        hidden_copy.start()

    def key_gradient():
        for zi in range(depth):
            lanes = slice(zi * part, (zi + 1) * part)
            term = t_mul(hidden_pair[:, lanes], d_lin[:, group_width:]).astype(BF16)
            kvs_part[zi, :, :, :, :, : 2 * HEAD_DIM] = term.reshape(
                2, 2, 2, model_rows, 2 * HEAD_DIM
            )

    def small_gradients():
        for copy in late_loads[6:]:
            copy.wait()
        lines[...] = jnp.zeros_like(lines)
        pairs[...] = jnp.zeros_like(pairs)
        bias = jnp.sum(d_lin[...].astype(F32), axis=0, keepdims=True)
        own_head = pl.ds(pl.multiple_of(place.x * HEAD_DIM, HEAD_DIM), HEAD_DIM)
        own_heads = pl.ds(pl.multiple_of(place.x * group_width, group_width), group_width)
        gain_one = jnp.zeros((1, model), F32)
        for x in range(2):
            normed, _ = normed_of(pair[x])
            gain_one = gain_one + jnp.sum(d_hidden[x] * normed, axis=0, keepdims=True)
        lines[0:1, :] = gain_one
        lines[1:2, own_heads] = bias[:, :group_width]
        lines[4:5, :] = gain_two[0:1]
        pairs[0:1, own_head] = bias[:, group_width : group_width + HEAD_DIM]
        pairs[1:2, own_head] = bias[:, group_width + HEAD_DIM :]
        chosen = lax.broadcasted_iota(jnp.int32, (key_width, model), 0)
        chosen = lax.div(chosen, share) * model_rows + lax.rem(chosen, share)
        chosen = (lax.broadcasted_iota(jnp.int32, (key_width, model), 1) == chosen).astype(BF16)
        spread = jnp.dot(pairs[...].astype(BF16), chosen, preferred_element_type=F32)
        lines[2:4, :] = spread[0:2]
        small = jnp.concatenate([lines[...], jnp.zeros((120, model), F32)], axis=0)
        small = small.T.astype(BF16)
        for zi in range(depth):
            kvs_part[zi, :, :, :, :, 2 * HEAD_DIM :] = small[
                zi * part : (zi + 1) * part
            ].reshape(2, 2, 2, model_rows, 128)

    def input_gradient():
        hidden_copy.wait_recv()
        normed, inv_one = normed_of(pair[place.x])
        scaled = (d_hidden[place.x] + h_far[...].astype(F32)) * vectors[0:1]
        input_grad[...] = d_middle[...] + inv_one * (
            scaled - normed * jnp.mean(scaled * normed, axis=-1, keepdims=True)
        )

    works = {
        "out": out_gradient,
        "delta": deltas,
        "turn": query_turn,
        "query": query_gradient,
        "key": key_turn,
        "hq": hidden_query,
        "hk": hidden_key,
        "kg": key_gradient,
        "Xq": r_q.swap,
        "Xs": r_s.swap,
        "small": small_gradients,
        "input": input_gradient,
        "down": down_copy.start,
    }
    jobs = {"o": r_o, "k": r_kv, "q": r_q, "s": r_s}
    follow_last(LAST_PLAN, works, depart, attend_wave, jobs)
    for job in (r_o, r_q, r_s):
        job.finish()
    for offset in range(1, count):
        origin = lax.rem(place.s + count - offset, count)
        block = wide_out.at[origin]
        remote(block, block, e_send.at[0], e_recv.at[offset], place.flip_c()).wait_recv()
    own_wide.wait()
    down_load.wait()
    down_copy.wait()
    down_out[...] = d_near[...].astype(F32) + d_far[...].astype(F32)
    hidden_copy.wait_send()
    for job in (r_kv, r_o, r_q, r_s):
        job.settle()
    for copy in sent:
        copy.wait_send()


def call_last(depth, collective_id, hbm, vmems, late):
    kv_all, pack_all, wide, down = hbm
    pair = late[6]
    count = 2 * depth
    _, rows, model = pair.shape
    model_rows = model // (4 * count)
    key_width, group_width = KV_HEADS * HEAD_DIM, GROUP * HEAD_DIM
    heads = (2, GROUP * rows, HEAD_DIM)
    lead = (depth, 2, 2, 2)
    kv_block, o_block = (rows, 2 * HEAD_DIM), (model_rows, model)
    blocks = [
        (model_rows, group_width),
        (model_rows, 2 * HEAD_DIM + 128),
    ]
    scratch = [
        pltpu.VMEM(kv_all.shape, BF16),
        pltpu.VMEM((2,) + pack_all.shape[1:], BF16),
        pltpu.VMEM(heads, F32),
        pltpu.VMEM(heads, F32),
        pltpu.VMEM((2 * rows, group_width + 2 * HEAD_DIM), BF16),
        pltpu.VMEM(lead + kv_block, BF16),
        pltpu.VMEM((2,) + kv_block, F32),
        pltpu.VMEM(lead + o_block, BF16),
    ]
    scratch += [pltpu.VMEM(lead + block, BF16) for block in blocks]
    scratch += [pltpu.VMEM(down.shape[1:], BF16)] * 2
    scratch += [
        pltpu.VMEM((2, rows, model), F32),
        pltpu.VMEM((model, 2 * HEAD_DIM), BF16),
        pltpu.VMEM(heads, BF16),
        pltpu.VMEM((rows, model), BF16),
        pltpu.VMEM((rows, model), BF16),
        pltpu.VMEM((8, model), F32),
        pltpu.VMEM((8, key_width), F32),
    ]
    scratch += [pltpu.VMEM(array.shape, array.dtype) for array in late]
    buffers, sems = Reduce.scratch(depth, True, o_block)
    scratch += buffers + sems
    for block in [kv_block] + blocks:
        buffers, sems = PairReduce.scratch(depth, block)
        scratch += buffers + sems
    scratch += [DMA((3 + depth,)), DMA((count,)), DMA((count,)), DMA((1,)), DMA((1,))]
    scratch += [DMA((2,)), DMA((2,)), DMA((len(late),))]
    any_, vmem = pl.BlockSpec(memory_space=pl.ANY), pl.BlockSpec(memory_space=pltpu.VMEM)
    return pl.pallas_call(
        functools.partial(last_kernel, depth),
        out_shape=[
            jax.ShapeDtypeStruct((rows, model), F32),
            jax.ShapeDtypeStruct((2,) + blocks[0], F32),
            jax.ShapeDtypeStruct((2,) + blocks[1], F32),
            jax.ShapeDtypeStruct(o_block, F32),
            jax.ShapeDtypeStruct(down.shape[1:], F32),
            jax.ShapeDtypeStruct(wide.shape, BF16),
        ],
        in_specs=[any_] * 4 + [vmem] * len(vmems) + [any_] * len(late),
        out_specs=[vmem] * 6,
        scratch_shapes=scratch,
        compiler_params=pltpu.CompilerParams(
            collective_id=collective_id, has_side_effects=True, vmem_limit_bytes=VMEM_JOINED
        ),
    )(*hbm, *vmems, *late)


def finish_kernel(few, plain, *refs):
    ins, refs = refs[: 4 + plain], refs[4 + plain :]
    outs, vectors, refs = refs[: 6 + plain], refs[6 + plain : 11 + plain], refs[11 + plain :]
    held, refs = refs[: 4 + plain], refs[4 + plain :]
    gate, up, query, key, value, in_sem, out_sem = refs
    loads = [
        pltpu.make_async_copy(source, target, in_sem.at[number])
        for number, (source, target) in enumerate(zip(ins, held))
    ]
    for copy in loads:
        copy.start()
    wide, down, q_in, kvs_in = held[:4]
    filled = wide.shape[3] // 4
    stores = []

    def store(source, number):
        copy = pltpu.make_async_copy(source, outs[number], out_sem.at[number])
        copy.start()
        stores.append(copy)

    loads[0].wait()
    for side, out in enumerate((gate, up)):
        for place in range(wide.shape[0]):
            block = wide[place, side].astype(F32)
            for owner in range(4):
                low = (4 * place + owner) * few
                out[:, low : low + few] = block[:, owner * filled : owner * filled + few]
        store(out, side)
    loads[1].wait()
    store(down.at[pl.ds(0, few)], 2)
    for number in range(plain):
        loads[4 + number].wait()
        store(held[4 + number], 6 + number)
    loads[2].wait()
    loads[3].wait()
    for g in range(KV_HEADS):
        width = q_in.shape[2]
        query[:, g * width : (g + 1) * width] = q_in[g]
        lanes = slice(g * HEAD_DIM, (g + 1) * HEAD_DIM)
        key[:, lanes] = kvs_in[g, :, :HEAD_DIM]
        value[:, lanes] = kvs_in[g, :, HEAD_DIM : 2 * HEAD_DIM]
    for number, source in enumerate((query, key, value)):
        store(source, 3 + number)
    rows_of = (kvs_in[0, :, 2 * HEAD_DIM :] + kvs_in[1, :, 2 * HEAD_DIM :]).T
    for number, out in enumerate(vectors):
        out[...] = rows_of[number : number + 1, : out.shape[1]]
    for copy in stores:
        copy.wait()


def call_finish(few, sizes, wide, down, q_grad, kvs_grad, plain):
    seq, _, rows, _ = wide.shape
    key_width = KV_HEADS * HEAD_DIM
    units = seq * 4 * few
    any_, vmem = pl.BlockSpec(memory_space=pl.ANY), pl.BlockSpec(memory_space=pltpu.VMEM)
    ins = (wide, down, q_grad, kvs_grad, *plain)
    made = [
        jax.ShapeDtypeStruct((rows, units), F32),
        jax.ShapeDtypeStruct((rows, units), F32),
        jax.ShapeDtypeStruct((rows, HEADS * HEAD_DIM), F32),
        jax.ShapeDtypeStruct((rows, key_width), F32),
        jax.ShapeDtypeStruct((rows, key_width), F32),
    ]
    out_shape = made[:2] + [jax.ShapeDtypeStruct((few, down.shape[1]), F32)] + made[2:]
    out_shape += [jax.ShapeDtypeStruct(array.shape, array.dtype) for array in plain]
    out_shape += [jax.ShapeDtypeStruct((1, size), F32) for size in sizes]
    return pl.pallas_call(
        functools.partial(finish_kernel, few, len(plain)),
        out_shape=out_shape,
        in_specs=[any_] * len(ins),
        out_specs=[any_] * (6 + len(plain)) + [vmem] * len(sizes),
        scratch_shapes=[pltpu.VMEM(array.shape, array.dtype) for array in (*ins, *made)]
        + [DMA((len(ins),)), DMA((6 + len(plain),))],
        compiler_params=pltpu.CompilerParams(vmem_limit_bytes=VMEM_LIMIT),
    )(*ins)


def begin_of(positions, lengths):
    ends = jnp.cumsum(lengths)
    starts = ends - lengths
    inside = (positions[:, None] >= starts[None, :]) & (positions[:, None] < ends[None, :])
    return jnp.sum(jnp.where(inside, starts[None, :], 0), axis=1)


def rope_tables(places, head_size):
    half_size = head_size // 2
    frequency = ROPE_BASE ** (-2.0 * jnp.arange(half_size, dtype=F32) / head_size)
    angles = places.astype(F32)[:, None] * frequency[None, :]
    return (jnp.cos(angles), jnp.sin(angles))


def rotate(vector, cosine, sine_table, direction):
    half_size = vector.shape[-1] // 2
    front_half = vector[..., :half_size]
    back_half = vector[..., half_size:]
    cosine = cosine[:, None, :]
    sine_table = direction * sine_table[:, None, :]
    return jnp.concatenate(
        [
            front_half * cosine - back_half * sine_table,
            back_half * cosine + front_half * sine_table,
        ],
        axis=-1,
    )


def norm_back(grad_normed, normed, inverse, gain_row):
    scaled = grad_normed * gain_row
    return inverse * (scaled - normed * jnp.mean(scaled * normed, axis=-1, keepdims=True))


def dot(left, right):
    return jnp.dot(left, right, preferred_element_type=F32)


def dot_t(left, right):
    return lax.dot_general(left, right, (((1,), (1,)), ((), ())), preferred_element_type=F32)


def t_dot(left, right):
    return lax.dot_general(left, right, (((0,), (0,)), ((), ())), preferred_element_type=F32)


def column(vector, rows):
    return jnp.pad(vector, (0, rows - vector.shape[0]))[:, None]


def shards_apart(
    tokens,
    cotangent,
    lengths,
    attn_gain,
    q_weight,
    q_bias,
    k_weight,
    k_bias,
    v_weight,
    v_bias,
    o_weight,
    mlp_gain,
    gate_weight,
    up_weight,
    down_weight,
):
    seq, fsdp = lax.axis_size("seq"), lax.axis_size("fsdp")
    devices = seq * fsdp
    depth = seq // 2
    rows, model = tokens.shape
    total = rows * devices
    key_width = KV_HEADS * HEAD_DIM
    query_width = HEADS * HEAD_DIM
    model_rows = q_weight.shape[0]
    units = gate_weight.shape[1] // seq
    first_row = lax.axis_index(AXES) * rows
    positions = first_row + jnp.arange(rows, dtype=jnp.int32)
    begin = begin_of(positions, lengths)
    cosine, sine_table = rope_tables(positions - begin, HEAD_DIM)
    score_scale = HEAD_DIM ** (-0.5)

    small = jnp.concatenate(
        [column(v, model_rows) for v in (attn_gain, q_bias, k_bias, v_bias, mlp_gain)]
        + [jnp.zeros((model_rows, 123), BF16)],
        axis=1,
    )
    pack = jnp.concatenate([q_weight, k_weight, v_weight, o_weight, small], axis=1)
    wide = jnp.stack([gate_weight, up_weight]).reshape(2, model_rows, seq, units)
    wide = wide.transpose(0, 2, 1, 3)
    pack_all, cot_all, wide_all, down_all = call_start(
        depth, 0, pack, cotangent, wide, down_weight
    )
    pack_all = pack_all.reshape(model, pack.shape[1])
    qkv_width = query_width + 2 * key_width
    w_qkv = pack_all[:, :qkv_width]
    w_out = pack_all[:, qkv_width : qkv_width + query_width]
    smalls = pack_all[:, qkv_width + query_width :].astype(F32)
    gain_one, b_query = smalls[:, 0], smalls[:, 1]
    gain_two = smalls[:, 4]
    kv_share = k_bias.shape[0]
    b_key = smalls[:, 2].reshape(devices, model_rows)[:, :kv_share].reshape(key_width)
    b_value = smalls[:, 3].reshape(devices, model_rows)[:, :kv_share].reshape(key_width)
    cot_all = cot_all.reshape(seq * rows, model)
    w_gate = wide_all[0].reshape(model, units)
    w_up = wide_all[1].reshape(model, units)
    w_down = down_all.reshape(units, model)

    inputs = tokens.astype(F32)
    inv_one = lax.rsqrt(jnp.mean(inputs * inputs, axis=-1, keepdims=True) + EPSILON)
    normed_one = inputs * inv_one
    hidden_one = (normed_one * gain_one).astype(BF16)
    lin = dot(hidden_one, w_qkv) + jnp.concatenate([b_query, b_key, b_value])
    queries = rotate(
        lin[:, :query_width].reshape(rows, HEADS, HEAD_DIM), cosine, sine_table, 1.0
    ).astype(BF16)
    queries = queries.transpose(1, 0, 2).reshape(KV_HEADS, GROUP * rows, HEAD_DIM)
    keys = rotate(
        lin[:, query_width : query_width + key_width].reshape(rows, KV_HEADS, HEAD_DIM),
        cosine,
        sine_table,
        1.0,
    ).reshape(rows, key_width)
    kv = jnp.concatenate([keys, lin[:, query_width + key_width :]], axis=1).astype(BF16)
    (kv_all,) = call_gathers(depth, 1, [True], [kv])
    kv_all = kv_all.reshape(total, 2 * key_width)
    all_keys, all_values = kv_all[:, :key_width], kv_all[:, key_width:]

    span = min(512, total)
    low = begin[0] // span
    high = (first_row + rows - 1) // span + 1
    info = jnp.stack([first_row, low, high]).astype(jnp.int32)
    begin_column = begin[:, None]
    mixed, lse = call_forward(span, info, begin_column, queries, all_keys, all_values)
    mixed_low = (
        mixed.reshape(HEADS, rows, HEAD_DIM)
        .transpose(1, 0, 2)
        .reshape(rows, query_width)
        .astype(BF16)
    )
    middle = inputs + dot(mixed_low, w_out)
    inv_two = lax.rsqrt(jnp.mean(middle * middle, axis=-1, keepdims=True) + EPSILON)
    normed_two = middle * inv_two
    hidden_two = (normed_two * gain_two).astype(BF16)

    (hidden_all,) = call_gathers(depth, 2, [False], [hidden_two])
    hidden_all = hidden_all.reshape(seq * rows, model)
    gate = dot(hidden_all, w_gate)
    up = dot(hidden_all, w_up)
    sigma = jax.nn.sigmoid(gate)
    silu = gate * sigma
    activated = (silu * up).astype(BF16)
    d_act = dot_t(cot_all, w_down)
    d_gate = (d_act * up * sigma * (1.0 + gate * (1.0 - sigma))).astype(BF16)
    d_up = (d_act * silu).astype(BF16)
    d_hidden_part = dot_t(d_gate, w_gate) + dot_t(d_up, w_up)
    out_part = dot(activated, w_down)
    shape = (depth, 2, rows, model)
    d_hidden_two, branch = call_reduces(
        depth,
        3,
        [False, False],
        [d_hidden_part.astype(BF16).reshape(shape), out_part.astype(BF16).reshape(shape)],
    )
    layer_out = (middle + branch).astype(BF16)
    gate_part = t_dot(hidden_all, d_gate).astype(BF16)
    up_part = t_dot(hidden_all, d_up).astype(BF16)
    down_part = t_dot(activated, cot_all).astype(BF16)

    gain_two_grad = jnp.sum(d_hidden_two * normed_two, axis=0)
    d_middle = cotangent.astype(F32) + norm_back(d_hidden_two, normed_two, inv_two, gain_two)

    d_branch = d_middle.astype(BF16)
    d_mixed = dot_t(d_branch, w_out).astype(BF16)
    d_mixed = (
        d_mixed.reshape(rows, HEADS, HEAD_DIM)
        .transpose(1, 0, 2)
        .reshape(KV_HEADS, GROUP * rows, HEAD_DIM)
    )
    d_query, d_kv_part = call_backward(
        span, info, begin_column, queries, all_keys, all_values, mixed, lse, d_mixed
    )
    (d_kv,) = call_reduces(
        depth, 4, [True], [d_kv_part.reshape(depth, 2, 2, 2, rows, 2 * key_width)]
    )
    d_query = d_query.reshape(HEADS, rows, HEAD_DIM).transpose(1, 0, 2)
    d_q = rotate(d_query * score_scale, cosine, sine_table, -1.0).reshape(rows, query_width)
    d_k = rotate(
        d_kv[:, :key_width].reshape(rows, KV_HEADS, HEAD_DIM) * score_scale,
        cosine,
        sine_table,
        -1.0,
    ).reshape(rows, key_width)
    d_lin = jnp.concatenate([d_q, d_k, d_kv[:, key_width:]], axis=1).astype(BF16)
    bias_grad = jnp.sum(d_lin.astype(F32), axis=0)
    d_hidden_one = dot_t(d_lin, w_qkv)
    gain_one_grad = jnp.sum(d_hidden_one * normed_one, axis=0)
    input_grad = d_middle + norm_back(d_hidden_one, normed_one, inv_one, gain_one)

    def spread(vector):
        parts = vector.reshape(devices, -1)
        return jnp.pad(parts, ((0, 0), (0, model_rows - parts.shape[1]))).reshape(model, 1)

    small_part = jnp.concatenate(
        [
            spread(gain_one_grad),
            spread(bias_grad[:query_width]),
            spread(bias_grad[query_width : query_width + key_width]),
            spread(bias_grad[query_width + key_width :]),
            spread(gain_two_grad),
            jnp.zeros((model, 123), F32),
        ],
        axis=1,
    )
    pack_part = jnp.concatenate(
        [
            t_dot(hidden_one, d_lin).astype(BF16),
            t_dot(mixed_low, d_branch).astype(BF16),
            small_part.astype(BF16),
        ],
        axis=1,
    ).reshape(depth, 2, 2, 2, model_rows, pack.shape[1])
    wide_part = jnp.stack([gate_part, up_part]).reshape(2, seq, fsdp, model_rows, units)
    down_part = down_part.reshape(fsdp, units // fsdp, model)
    pack_grad, wide_grad, down_grad = call_end(depth, 5, pack_part, wide_part, down_part)
    wide_grad = wide_grad.transpose(1, 2, 0, 3).reshape(2, model_rows, seq * units).astype(F32)
    small_grad = pack_grad[:, qkv_width + query_width :]
    return (
        layer_out,
        input_grad,
        small_grad[:, 0],
        pack_grad[:, :query_width],
        small_grad[:, 1],
        pack_grad[:, query_width : query_width + key_width],
        small_grad[:kv_share, 2],
        pack_grad[:, query_width + key_width : qkv_width],
        small_grad[:kv_share, 3],
        pack_grad[:, qkv_width : qkv_width + query_width],
        small_grad[:, 4],
        wide_grad[0],
        wide_grad[1],
        down_grad,
    )


def shards_joined(
    tokens,
    cotangent,
    lengths,
    attn_gain,
    q_weight,
    q_bias,
    k_weight,
    k_bias,
    v_weight,
    v_bias,
    o_weight,
    mlp_gain,
    gate_weight,
    up_weight,
    down_weight,
):
    seq, fsdp = lax.axis_size("seq"), lax.axis_size("fsdp")
    devices = seq * fsdp
    depth = seq // 2
    rows, model = tokens.shape
    key_width = KV_HEADS * HEAD_DIM
    model_rows = q_weight.shape[0]
    kv_share = k_bias.shape[0]
    small = jnp.stack(
        [jnp.pad(v, (0, model_rows - v.shape[0])) for v in (attn_gain, q_bias, k_bias, v_bias, mlp_gain)],
        axis=1,
    )
    small = jnp.pad(small, ((0, 0), (0, 123)))
    few = down_weight.shape[0]
    filled = fsdp * (few + -few % 16)
    steps = np.arange(HEAD_DIM) % (HEAD_DIM // 2)
    frequency = jnp.asarray((ROPE_BASE ** (-2.0 * steps / HEAD_DIM)).astype(np.float32)[None, :])
    (
        pack_all,
        o_all,
        kv_all,
        cot_all,
        wide_all,
        down_all,
        hidden_all,
        queries,
        mixed,
        lse,
        middle,
        hidden_pair,
        mixed_low,
        pair,
        angles,
        begin,
        vectors,
    ) = call_head(
        depth,
        6,
        (o_weight,),
        (
            q_weight,
            k_weight,
            v_weight,
            small,
            gate_weight,
            up_weight,
            down_weight,
            tokens,
            cotangent,
            frequency,
        ),
        lengths,
    )
    layer_out, d_middle, d_mixed, d_branch, gain_two_grad, down_part, wide_part = call_middle(
        depth,
        7,
        (
            hidden_all,
            cot_all,
            wide_all.reshape(2, seq, 2, 2, model_rows, filled),
            down_all.reshape(filled, model),
            o_all,
        ),
        (middle, cotangent, vectors),
    )
    input_grad, q_grad, kvs_grad, o_grad, down_grad, wide_grad = call_last(
        depth,
        8,
        (kv_all, pack_all, wide_part, down_part),
        (d_mixed, angles, begin, vectors, gain_two_grad),
        (queries, mixed, lse, mixed_low, d_branch, hidden_pair, pair, d_middle),
    )
    sizes = (model_rows, model_rows, kv_share, kv_share, model_rows)
    gate_grad, up_grad, down_grad, q_grad, k_grad, v_grad, *rest = call_finish(
        few, sizes, wide_grad, down_grad, q_grad, kvs_grad, (layer_out, input_grad, o_grad)
    )
    layer_out, input_grad, o_grad = rest[:3]
    small_grad = [vector.reshape(-1) for vector in rest[3:]]
    return (
        layer_out,
        input_grad,
        small_grad[0],
        q_grad,
        small_grad[1],
        k_grad,
        small_grad[2],
        v_grad,
        small_grad[3],
        o_grad,
        small_grad[4],
        gate_grad,
        up_grad,
        down_grad,
    )


def shards(*arguments):
    model_rows, rows = arguments[4].shape[0], arguments[0].shape[0]
    if model_rows % 16 == 0 and rows % 128 == 0 and lax.axis_size("seq") == 8:
        return shards_joined(*arguments)
    return shards_apart(*arguments)


def solution(mesh):
    matrix, vector = P(AXES, None), P(AXES)
    in_specs = (
        matrix,
        matrix,
        P(),
        vector,
        matrix,
        vector,
        matrix,
        vector,
        matrix,
        vector,
        matrix,
        vector,
        matrix,
        matrix,
        matrix,
    )
    out_specs = (
        matrix,
        matrix,
        vector,
        matrix,
        vector,
        matrix,
        vector,
        matrix,
        vector,
        matrix,
        vector,
        matrix,
        matrix,
        matrix,
    )
    return jax.shard_map(shards, mesh=mesh, in_specs=in_specs, out_specs=out_specs, check_vma=False)
```

profile of v0, /device:TPU:0, one launch (start us, length us, event | category | flops | bytes accessed | tf_op | source)
XLA Modules:
  0.0 353.0 jit_solution(7562242581722824640)
XLA Ops:
  0.6 0.7 pad_bitcast_fusion
  1.3 0.7 stack.23
  2.0 0.1 copy.35
  2.1 0.6 pad.13.refs_4_
  2.8 148.8 %shard_map.263 = (bf16[4,2,2,2,48,1152]{5,4,3,2,1,0:T(8,128)(2,1)}, bf16[4,2,2,2,48,1536]{5,4,3,2,1,0:T(8,128)(2,1)}, bf16[4,2,2,2,128,256]{5,4,3,2,1,0:T(8,128)...) custom-call(bf16[48,1536]{1,0:T(8,128)(2,1)} %refs_0_.1, ...), custom_call_target="tpu_custom_call" | custom-call | tf_op jit(solution)/shard_map/pallas_call | solution.py:1728
  151.6 104.4 %shard_map.264 = (bf16[128,1536]{1,0:T(8,128)(2,1)}, f32[128,1536]{1,0:T(8,128)}, bf16[2,768,128]{2,1,0:T(8,128)(2,1)}, bf16[128,1536]{1,0:T(8,128)(2,1)}, f32[8...) custom-call(bf16[4,2,128,1536]{3,2,1,0:T(8,128)(2,1)} %get-tuple-element.60.refs_0_, ...), custom_call_target="tpu_custom_call" | custom-call | tf_op jit(solution)/shard_map/pallas_call | solution.py:2005
  255.9 91.0 %shard_map.265 = (f32[128,1536]{1,0:T(8,128)}, f32[2,48,768]{2,1,0:T(8,128)}, f32[2,48,384]{2,1,0:T(8,128)}, f32[48,1536]{1,0:T(8,128)}, f32[288,1536]{1,0:T(8,128)}, /*index=5*/bf16[8,2,48,1152]{3,2,1,0:T(8,128)(2,1)}) custom-call(bf16[4,2,2,2,128,256]{5,4,3,2,1,0:T(8,128)(2,1)} %get-tuple-element.58.refs_0_, ...), custom_call_target="tpu_custom_call" | custom-call | tf_op jit(solution)/shard_map/pallas_call | solution.py:2376
  346.9 5.6 %shard_map.266 = (f32[48,8960]{1,0:T(8,128)}, f32[48,8960]{1,0:T(8,128)}, f32[280,1536]{1,0:T(8,128)}, f32[48,1536]{1,0:T(8,128)}, f32[48,256]{1,0:T(8,128)}, /*...) custom-call(bf16[8,2,48,1152]{3,2,1,0:T(8,128)(2,1)} %get-tuple-elem, ...), custom_call_target="tpu_custom_call" | custom-call | tf_op jit(solution)/shard_map/pallas_call | solution.py:2461
where the time goes:
time: 360 us; the launch traced here: 353 us
  Pallas kernels  350 us (97%)
    pallas_call x1, Pallas kernels, call_head(): pl.pallas_call(functools.partial(head_kernel, depth), out_shape=outs, in_...  149 us
    pallas_call x1, Pallas kernels, call_middle(): pl.pallas_call(functools.partial(middle_kernel, depth), out_shape=[jax.Sh...  104 us
    pallas_call x1, Pallas kernels, call_last(): pl.pallas_call(functools.partial(last_kernel, depth), out_shape=[jax.Shap...  91 us

commit v1 on v0

--- a/solution.py
+++ b/solution.py
@@ -1388,7 +1388,7 @@
 
 
 def head_kernel(depth, *refs):
-    (o_own, q_own, k_own, v_own, small_own, gate_own, up_own, down_own) = refs[:8]
+    (o_own, gate_far, up_far, down_far, q_own, k_own, v_own, small_own) = refs[:8]
     (tokens, cot, frequency, lengths) = refs[8:HEAD_INS]
     (
         pack_out,
@@ -1413,7 +1413,8 @@
     pack_all, o_all, kv_all, kv_own, hidden_two, lin, m_acc, l_acc, o_acc = rest[:9]
     pack, wide, down, mixed_pair, mixed_far, spread = rest[9:15]
     queries, mixed, lse, middle, hidden_pair, mixed_low, pair, angles = rest[15:23]
-    sems = list(rest[23:])
+    gate_own, up_own, down_own = rest[23:26]
+    sems = list(rest[26:])
 
     def take(count):
         taken = sems[:count]
@@ -1446,7 +1447,15 @@
     g_hidden = Gather(place, False, hidden_two, hidden_out, take(line_need))
     x_wide = Exchange(place, wide, wide_out, take(len(Exchange.semaphores(depth))))
     x_down = Quarter(place, down, down_out, take(len(Quarter.semaphores())))
-    out_sem, x_send, x_recv = take(3)
+    out_sem, x_send, x_recv, far_sem = take(4)
+    far_loads = [
+        pltpu.make_async_copy(source, target, far_sem.at[number])
+        for number, (source, target) in enumerate(
+            ((gate_far, gate_own), (up_far, up_own), (down_far, down_own))
+        )
+    ]
+    for copy in far_loads:
+        copy.start()
 
     g_pack.begin()
     token_copy = remote(
@@ -1465,6 +1474,8 @@
     inputs = tokens[...].astype(F32)
 
     def pack_wide():
+        for copy in far_loads[:2]:
+            copy.wait()
         for side, source in enumerate((gate_own, up_own)):
             for to in range(count):
                 parts = []
@@ -1476,6 +1487,7 @@
         locals_[2].start()
 
     def tables():
+        far_loads[2].wait()
         down[...] = jnp.concatenate(
             [down_own[...], jnp.zeros((filled - few, model), BF16)], axis=0
         )
@@ -1669,8 +1681,8 @@
 
 
 def call_head(depth, collective_id, hbm, vmems, lengths):
-    (o_own,) = hbm
-    q_own, k_own, v_own, small_own, gate_own, _, down_own, tokens, cot = vmems[:9]
+    o_own, gate_own, _, down_own = hbm
+    q_own, k_own, v_own, small_own, tokens, cot = vmems[:6]
     count = 2 * depth
     few = down_own.shape[0]
     filled = -(-few // 16) * 16
@@ -1720,15 +1732,16 @@
         pltpu.VMEM((8, key_width), F32),
     ]
     scratch += [pltpu.VMEM(out.shape, out.dtype) for out in outs[7:15]]
+    scratch += [pltpu.VMEM(array.shape, BF16) for array in hbm[1:]]
     scratch += PairGather.semaphores(depth) + Gather.semaphores(depth, True)
     scratch += PairGather.semaphores(depth)
     scratch += Gather.semaphores(depth, False, True) + Gather.semaphores(depth, False)
     scratch += Exchange.semaphores(depth) + Quarter.semaphores()
-    scratch += [DMA((11,)), DMA((2,)), DMA((2,))]
+    scratch += [DMA((11,)), DMA((2,)), DMA((2,)), DMA((3,))]
     return pl.pallas_call(
         functools.partial(head_kernel, depth),
         out_shape=outs,
-        in_specs=[any_] + [vmem] * len(vmems) + [pl.BlockSpec(memory_space=pltpu.SMEM)],
+        in_specs=[any_] * len(hbm) + [vmem] * len(vmems) + [pl.BlockSpec(memory_space=pltpu.SMEM)],
         out_specs=[any_] * 15 + [vmem] * 2,
         scratch_shapes=scratch,
         compiler_params=pltpu.CompilerParams(
@@ -2768,15 +2781,12 @@
     ) = call_head(
         depth,
         6,
-        (o_weight,),
+        (o_weight, gate_weight, up_weight, down_weight),
         (
             q_weight,
             k_weight,
             v_weight,
             small,
-            gate_weight,
-            up_weight,
-            down_weight,
             tokens,
             cotangent,
             frequency,

time: 360 us -> 359 us (level)
  no operation moved by 1% of the time
where the time goes in v1:
time: 359 us; the launch traced here: 352 us
  Pallas kernels  349 us (97%)
    pallas_call x1, Pallas kernels, call_head(): pl.pallas_call(functools.partial(head_kernel, depth), out_shape=outs, in_...  148 us
    pallas_call x1, Pallas kernels, call_middle(): pl.pallas_call(functools.partial(middle_kernel, depth), out_shape=[jax.Sh...  104 us
    pallas_call x1, Pallas kernels, call_last(): pl.pallas_call(functools.partial(last_kernel, depth), out_shape=[jax.Shap...  91 us

profile of v1, /device:TPU:0, one launch (start us, length us, event | category | flops | bytes accessed | tf_op | source)
XLA Modules:
  0.0 352.3 jit_solution(7868774518740122932)
XLA Ops:
  0.6 0.7 pad_bitcast_fusion
  1.3 0.7 stack.23
  2.0 0.1 copy.35
  2.1 0.6 pad.13.refs_7_
  2.8 148.1 %shard_map.263 = (bf16[4,2,2,2,48,1152]{5,4,3,2,1,0:T(8,128)(2,1)}, bf16[4,2,2,2,48,1536]{5,4,3,2,1,0:T(8,128)(2,1)}, bf16[4,2,2,2,128,256]{5,4,3,2,1,0:T(8,128)...) custom-call(bf16[48,1536]{1,0:T(8,128)(2,1)} %refs_0_.1, ...), custom_call_target="tpu_custom_call" | custom-call | tf_op jit(solution)/shard_map/pallas_call | solution.py:1741
  150.9 104.4 %shard_map.264 = (bf16[128,1536]{1,0:T(8,128)(2,1)}, f32[128,1536]{1,0:T(8,128)}, bf16[2,768,128]{2,1,0:T(8,128)(2,1)}, bf16[128,1536]{1,0:T(8,128)(2,1)}, f32[8...) custom-call(bf16[4,2,128,1536]{3,2,1,0:T(8,128)(2,1)} %get-tuple-element.60.refs_0_, ...), custom_call_target="tpu_custom_call" | custom-call | tf_op jit(solution)/shard_map/pallas_call | solution.py:2018
  255.2 91.0 %shard_map.265 = (f32[128,1536]{1,0:T(8,128)}, f32[2,48,768]{2,1,0:T(8,128)}, f32[2,48,384]{2,1,0:T(8,128)}, f32[48,1536]{1,0:T(8,128)}, f32[288,1536]{1,0:T(8,128)}, /*index=5*/bf16[8,2,48,1152]{3,2,1,0:T(8,128)(2,1)}) custom-call(bf16[4,2,2,2,128,256]{5,4,3,2,1,0:T(8,128)(2,1)} %get-tuple-element.58.refs_0_, ...), custom_call_target="tpu_custom_call" | custom-call | tf_op jit(solution)/shard_map/pallas_call | solution.py:2389
  346.2 5.6 %shard_map.266 = (f32[48,8960]{1,0:T(8,128)}, f32[48,8960]{1,0:T(8,128)}, f32[280,1536]{1,0:T(8,128)}, f32[48,1536]{1,0:T(8,128)}, f32[48,256]{1,0:T(8,128)}, /*...) custom-call(bf16[8,2,48,1152]{3,2,1,0:T(8,128)(2,1)} %get-tuple-elem, ...), custom_call_target="tpu_custom_call" | custom-call | tf_op jit(solution)/shard_map/pallas_call | solution.py:2474
